TPU v7x, 128 devices: a whole 4x4x4 slice. The times are simulated.
128 devices in a mesh: batch: 4 (over x_lo, core), patch: 32 (over y, z, x_hi).
Axes of the slice: x: 4 (x_hi: 2, x_lo: 2; x = x_hi * 2 + x_lo), y: 4, z: 4, core: 2. Of those that a mesh axis runs over, the one named last changes fastest.
Arguments:
- latent: bfloat16 [512, 64, 1280], P(('batch', 'patch')), parts along dimension 0, may hold values from -30 to 30
- gn_gain: float32 [1280], replicated, may hold values from 0.1 to 1.9
- w_query: bfloat16 [1280, 640], replicated, may hold values from -0.15625 to 0.15625
- w_key: bfloat16 [1280, 640], replicated, may hold values from -0.15625 to 0.15625
- w_value: bfloat16 [1280, 640], replicated, may hold values from -0.15625 to 0.15625
- w_out: bfloat16 [640, 1280], replicated, may hold values from -0.25 to 0.25
- stale_keys: bfloat16 [32768, 640], P(('batch', 'patch')), parts along dimension 0, may hold values from -150 to 150
- stale_values: bfloat16 [32768, 640], P(('batch', 'patch')), parts along dimension 0, may hold values from -5 to 5
- gn2_gain: float32 [1280], replicated, may hold values from 0.1 to 1.9
- conv_weight: bfloat16 [9, 1280, 640], replicated, may hold values from -0.0546875 to 0.0546875
- time_shift: float32 [2560], P('batch'), parts along dimension 0, may hold values from -4 to 4
Outputs:
- result: bfloat16 [512, 64, 640], P(('batch', 'patch')), parts along dimension 0
- fresh_keys: bfloat16 [32768, 640], P(('batch', 'patch')), parts along dimension 0
- fresh_values: bfloat16 [32768, 640], P(('batch', 'patch')), parts along dimension 0
There are 4 independent parts, one for each index of `batch`. A program takes and returns all parts, laid end to end along the dimension named above; an argument that names none is the same for every part. Nothing has to cross between parts.
All inputs are finite; a program needn't handle non-finite values.
Results may differ from a plain program's by a relative error of at most 0.005.
The roundings to bfloat16 on the way count: a program that leaves them out, or rounds other values in their place, can miss the bound.
Values may be sent and summed in bfloat16 or wider, within the bound.
No kernel may reach another device: no remote copies, remote signals or barrier semaphores. Data moves between devices by JAX's collectives and lax.ppermute only.
A program may use at most 128 MiB of HBM per device.

v0:
```python
import functools

import jax
import jax.numpy as jnp
from jax import lax
from jax.experimental import pallas as pl
from jax.experimental.pallas import tpu as pltpu
from jax.sharding import PartitionSpec as P

HEAD = 64
GROUPS = 32
LANES = 128
NY, NZ, NX = 4, 4, 2
EPS = 1e-05
BF = jnp.bfloat16
F32 = jnp.float32


def shifted(x, dy, dz, dx):
    pairs = []
    for y in range(NY):
        for z in range(NZ):
            for c in range(NX):
                to = (((y + dy) % NY) * NZ + (z + dz) % NZ) * NX + (c + dx) % NX
                pairs.append(((y * NZ + z) * NX + c, to))
    return lax.ppermute(x, "patch", pairs)


def members_of(channels, lead, offset):
    width = channels // GROUPS
    shape = (channels, LANES) if lead else (LANES, channels)
    chan = lax.broadcasted_iota(jnp.int32, shape, 0 if lead else 1)
    group = lax.broadcasted_iota(jnp.int32, shape, 1 if lead else 0) - offset
    inside = (chan >= group * width) & (chan < group * width + width)
    return jnp.where(inside, 1.0, 0.0).astype(BF)


def exact_dot(row, ones):
    at = lax.broadcasted_iota(jnp.int32, (16, row.shape[1]), 0)
    rest, cut = row, jnp.zeros((16, row.shape[1]), F32)
    for piece in range(3):
        part = rest.astype(BF).astype(F32)
        rest = rest - part
        cut = jnp.where(at == piece, part, cut)
    return jnp.sum(
        jnp.dot(cut.astype(BF), ones, preferred_element_type=F32), axis=0, keepdims=True
    )


def local_stats(x, peers):
    rows, channels = x.shape
    count = rows * (channels // GROUPS)
    total = jnp.sum(x, axis=0, keepdims=True)
    mean = exact_dot(total, members_of(channels, True, 0)) / count
    center = exact_dot(mean, members_of(channels, False, 0))
    squares = jnp.sum(jnp.square(x - center), axis=0, keepdims=True)
    spread = exact_dot(squares, members_of(channels, True, GROUPS))
    return jnp.broadcast_to(mean + spread, (peers, LANES))


def combined(stats, channels, count):
    peers = stats.shape[0]
    total = jnp.sum(stats, axis=0, keepdims=True)
    mean = total / peers
    between = jnp.sum(jnp.square(stats - mean), axis=0, keepdims=True) * count
    lead = members_of(channels, False, 0)
    center = exact_dot(mean, lead)
    spread = exact_dot(between, lead) + exact_dot(total, members_of(channels, False, GROUPS))
    return center, lax.rsqrt(spread / (count * peers) + EPS)


def full(shape):
    return pl.BlockSpec(shape, lambda *_: (0,) * len(shape))


HBM = pl.BlockSpec(memory_space=pltpu.HBM)
VMEM = pl.BlockSpec(memory_space=pltpu.VMEM)


def halves(src, dst, sems, first):
    size = src.shape[0] // 2
    return [
        pltpu.make_async_copy(
            src.at[i * size : (i + 1) * size], dst.at[i * size : (i + 1) * size], sems.at[first + i]
        )
        for i in range(2)
    ]


def stats_kernel(x_ref, k_ref, v_ref, wq, wk, wv, out_ref, old_ref, wq_out, wk_out, wv_out, held, sems):
    rows = k_ref.shape[0]
    copies = halves(x_ref, held, sems, 0)
    copies.append(pltpu.make_async_copy(k_ref, old_ref.at[0:rows], sems.at[2]))
    copies.append(pltpu.make_async_copy(v_ref, old_ref.at[rows : 2 * rows], sems.at[3]))
    for i, (src, dst) in enumerate(((wq, wq_out), (wk, wk_out), (wv, wv_out))):
        copies += halves(src, dst, sems, 4 + 2 * i)
    for copy in copies:
        copy.start()
    for copy in copies[:2]:
        copy.wait()
    out_ref[...] = local_stats(held[...].astype(F32), out_ref.shape[0])
    for copy in copies[2:]:
        copy.wait()


def norm_stats(x, keys, values, weights, peers):
    rows, width = keys.shape
    return pl.pallas_call(
        stats_kernel,
        in_specs=[HBM] * 6,
        out_specs=[VMEM] * 5,
        out_shape=[
            jax.ShapeDtypeStruct((peers, LANES), F32),
            jax.ShapeDtypeStruct((2 * rows, width), BF),
        ]
        + [pltpu.VMEM(w.shape, w.dtype) for w in weights],
        scratch_shapes=[pltpu.VMEM(x.shape, x.dtype), pltpu.SemaphoreType.DMA((10,))],
        name="norm_stats",
        compiler_params=pltpu.CompilerParams(vmem_limit_bytes=60030976),
        cost_estimate=pl.CostEstimate(flops=4 * x.size, bytes_accessed=2 * x.size, transcendentals=0),
    )(x, keys, values, *weights)


def project_kernel(stats_ref, x_ref, gain_ref, wq, wk, wv, q_ref, k_ref, v_ref, both_ref):
    rows, channels = x_ref.shape
    center, scale = combined(stats_ref[...], channels, rows * (channels // GROUPS))
    gain = gain_ref[...].reshape(1, channels)
    normed = ((x_ref[...].astype(F32) - center) * scale * gain).astype(BF)
    for i, (w_ref, o_ref) in enumerate(((wq, q_ref), (wk, k_ref), (wv, v_ref))):
        found = jnp.dot(normed, w_ref[...], preferred_element_type=F32).astype(BF)
        o_ref[...] = found
        if i > 0:
            both_ref[(i - 1) * rows : i * rows, :] = found


def project(stats, x, gain, wq, wk, wv):
    rows, channels = x.shape
    width = wq.shape[1]
    return pl.pallas_call(
        project_kernel,
        in_specs=[VMEM] * 6,
        out_specs=[VMEM] * 4,
        out_shape=[jax.ShapeDtypeStruct((rows, width), BF)] * 3
        + [jax.ShapeDtypeStruct((2 * rows, width), BF)],
        name="project",
        compiler_params=pltpu.CompilerParams(vmem_limit_bytes=24 * 2**20),
        cost_estimate=pl.CostEstimate(
            flops=6 * rows * channels * width,
            bytes_accessed=6 * channels * width,
            transcendentals=0,
        ),
    )(stats, x, gain, wq, wk, wv)


def attend_pair(queries, keys, values):
    rows = queries.shape[0]
    first = lax.broadcasted_iota(jnp.int32, (rows, LANES), 1) < HEAD
    scaled = queries * BF(0.125)
    none = jnp.zeros_like(scaled)
    found = []
    for mine in (jnp.where(first, scaled, none), jnp.where(first, none, scaled)):
        scores = lax.dot_general(
            mine, keys, (((1,), (1,)), ((), ())), preferred_element_type=F32
        )
        top = jnp.max(scores, axis=1, keepdims=True)
        weights = jnp.exp(scores - top).astype(BF)
        both = jnp.dot(weights, values, preferred_element_type=F32)
        found.append((both[:, :LANES], jnp.broadcast_to(top, (rows, LANES)), both[:, LANES:]))
    return first, found


def attend_kernel(plan, start, final, waits, carry, unroll, *refs):
    count, rows_of = plan
    refs = list(refs)
    take = lambda n: [refs.pop(0) for _ in range(n)]
    queries, sources = take(count), take(2 * len(rows_of))
    state = take(3) if start else None
    take(waits)
    brought = take(1 if carry else 0)
    outs = take(count if final else 3)
    copies = []
    if carry:
        (kept,), (sems,) = take(1), take(1)
        copies = [
            pltpu.make_async_copy(brought[0].at[i], kept.at[i], sems.at[i]) for i in range(kept.shape[0])
        ]
        for copy in copies:
            copy.start()
    rows, width = queries[0].shape
    lane = lax.broadcasted_iota(jnp.int32, (rows, LANES), 1)
    ones = jnp.ones((rows, LANES), BF)
    if final:
        for o_ref in outs:
            o_ref[:, width:] = jnp.zeros((rows, o_ref.shape[1] - width), BF)

    def pair(j, carried):
        cols = pl.ds(pl.multiple_of(j * LANES, LANES), LANES)
        keys, values = [], []
        for i, (key_row, value_row) in enumerate(rows_of):
            keys.append(sources[2 * i][key_row * rows : (key_row + 1) * rows, cols])
            value = sources[2 * i + 1][value_row * rows : (value_row + 1) * rows, cols]
            values.append(jnp.concatenate([value, ones], axis=1))
        keys, values = jnp.concatenate(keys, axis=0), jnp.concatenate(values, axis=0)
        for band, q_ref in enumerate(queries):
            first, found = attend_pair(q_ref[:, cols], keys, values)
            at = slice(band * rows, (band + 1) * rows)
            summed, top, total = (jnp.where(first, found[0][n], found[1][n]) for n in range(3))
            if state is not None:
                old_top = state[1][at, cols]
                new_top = jnp.maximum(top, old_top)
                part, old_part = jnp.exp(top - new_top), jnp.exp(old_top - new_top)
                top = new_top
                total = part * total + old_part * state[2][at, cols]
                summed = part * summed + old_part * state[0][at, cols]
            if not final:
                for out_ref, value in zip(outs, (summed, top, total)):
                    out_ref[at, cols] = value
                continue
            outs[band][:, cols] = (summed / total).astype(BF)
            level = top + jnp.log(total)
            swapped = pltpu.roll(level, HEAD, 1)
            row_level = (jnp.where(first, level, swapped), jnp.where(first, swapped, level))
            extra = outs[band][:, width : width + LANES]
            for h in range(2):
                rest = row_level[h]
                for piece in range(3):
                    part = rest.astype(BF)
                    rest = rest - part.astype(F32)
                    extra = jnp.where(lane == 2 * j + h + 10 * piece, part, extra)
            outs[band][:, width : width + LANES] = extra
        return carried

    lax.fori_loop(0, width // LANES, pair, 0, unroll=unroll)
    for copy in copies:
        copy.wait()


def attend(name, queries, blocks, state=None, final=False, after=(), carry=None, weight=16, extra=1, unroll=False):
    rows, width = queries[0].shape
    count = len(queries)
    sources = []
    for keys, _, values, _ in blocks:
        sources += [keys, values]
    plan = (count, [(key_row, value_row) for _, key_row, _, value_row in blocks])
    if final:
        out_shape = [jax.ShapeDtypeStruct((rows, width + extra * LANES), BF)] * count
    else:
        out_shape = [jax.ShapeDtypeStruct((count * rows, width), F32)] * 3
    scratch, carried = [], []
    if carry is not None:
        out_shape.append(pltpu.VMEM(carry.shape, carry.dtype))
        scratch.append(pltpu.SemaphoreType.DMA((carry.shape[0],)))
        carried.append(carry)
    state = tuple(state or ())
    return pl.pallas_call(
        functools.partial(attend_kernel, plan, bool(state), final, len(after), carry is not None, unroll),
        in_specs=[VMEM] * (count + len(sources) + len(state))
        + [pl.BlockSpec(memory_space=pl.ANY)] * len(after)
        + [HBM] * len(carried),
        out_specs=[VMEM] * len(out_shape),
        out_shape=out_shape,
        scratch_shapes=scratch,
        name=name,
        compiler_params=pltpu.CompilerParams(vmem_limit_bytes=24 * 2**20),
        cost_estimate=pl.CostEstimate(
            flops=weight * count * rows * len(blocks) * rows * width,
            bytes_accessed=weight * rows * LANES,
            transcendentals=0,
        ),
    )(*queries, *sources, *state, *after, *carried)


def merge_kernel(p0, p1, p2, p3, x_ref, w_ref, hidden_ref, stats_ref):
    width = w_ref.shape[0]
    lane = lax.broadcasted_iota(jnp.int32, (LANES, width), 0)
    chan = lax.broadcasted_iota(jnp.int32, (LANES, width), 1)
    spread = jnp.zeros((LANES, width), F32)
    for piece in range(3):
        head = lane - 10 * piece
        inside = (head >= 0) & (head < 10) & (chan >= head * HEAD) & (chan < head * HEAD + HEAD)
        spread = jnp.where(inside, 1.0, spread)
    spread = spread.astype(BF)
    parts = (p0, p1, p2, p3)
    levels = [jnp.dot(p[:, width : width + LANES], spread, preferred_element_type=F32) for p in parts]
    top = functools.reduce(jnp.maximum, levels)
    shares = [jnp.exp(level - top) for level in levels]
    total = functools.reduce(jnp.add, shares)
    summed = functools.reduce(
        jnp.add, [s * p[:, :width].astype(F32) for s, p in zip(shares, parts)]
    )
    attended = (summed / total).astype(BF)
    hidden = x_ref[...].astype(F32) + jnp.dot(attended, w_ref[...], preferred_element_type=F32)
    hidden_ref[...] = hidden
    stats_ref[...] = local_stats(hidden, stats_ref.shape[0])


def merge(parts, x, w_out, peers):
    rows, channels = x.shape
    return pl.pallas_call(
        merge_kernel,
        out_shape=[
            jax.ShapeDtypeStruct((rows, channels), F32),
            jax.ShapeDtypeStruct((peers, LANES), F32),
        ],
        name="merge_project",
        compiler_params=pltpu.CompilerParams(vmem_limit_bytes=24 * 2**20),
        cost_estimate=pl.CostEstimate(
            flops=2 * rows * w_out.size, bytes_accessed=2 * w_out.size, transcendentals=0
        ),
    )(*parts, x, w_out)


def conv_kernel(stats_ref, hidden_ref, above_ref, below_ref, gain_ref, w_ref, shift_ref, out_ref, moved):
    own = lax.axis_index("patch")
    last = lax.axis_size("patch") - 1
    rows, channels = hidden_ref.shape
    cols = above_ref.shape[0]
    width = out_ref.shape[1]
    center, scale = combined(stats_ref[...], channels, rows * (channels // GROUPS))
    gain = gain_ref[...].reshape(1, channels)
    col = lax.broadcasted_iota(jnp.int32, (cols, channels), 0)
    pieces = [(above_ref, 0, own != 0)]
    pieces += [(hidden_ref, i, None) for i in range(rows // cols)]
    pieces += [(below_ref, 0, own != last)]
    for place, (ref, part, kept) in enumerate(pieces):
        v = (ref[part * cols : (part + 1) * cols, :] - center) * scale * gain
        v = v / (1.0 + jnp.exp(-v))
        if kept is not None:
            v = jnp.where(kept, v, 0.0)
        to = slice(place * cols, (place + 1) * cols)
        left = jnp.where(col == 0, 0.0, pltpu.roll(v, 1, 0))
        right = jnp.where(col == cols - 1, 0.0, pltpu.roll(v, cols - 1, 0))
        for tap, value in enumerate((left, v, right)):
            moved[to, tap * channels : (tap + 1) * channels] = value.astype(BF)
    total = hidden_ref[:, :width] + shift_ref[...].reshape(1, width)
    for tap in range(3):
        window = moved[tap * cols : tap * cols + rows, :]
        taps = w_ref[3 * tap : 3 * tap + 3].reshape(3 * channels, width)
        total = total + jnp.dot(window, taps, preferred_element_type=F32)
    out_ref[...] = total.astype(BF)


def convolve(stats, hidden, above, below, gain, weight, shift):
    rows, channels = hidden.shape
    cols = above.shape[0]
    width = weight.shape[2]
    return pl.pallas_call(
        conv_kernel,
        in_specs=[VMEM] * 7,
        out_specs=VMEM,
        out_shape=jax.ShapeDtypeStruct((rows, width), BF),
        scratch_shapes=[pltpu.VMEM((rows + 2 * cols, 3 * channels), BF)],
        name="norm_convolve",
        compiler_params=pltpu.CompilerParams(vmem_limit_bytes=24 * 2**20),
        cost_estimate=pl.CostEstimate(
            flops=2 * rows * weight.size, bytes_accessed=2 * weight.size, transcendentals=0
        ),
    )(stats, hidden, above, below, gain, weight, shift)


def everyones(stats):
    return lax.all_to_all(stats, "patch", 0, 0, tiled=True)


def shards(
    latent,
    gn_gain,
    w_query,
    w_key,
    w_value,
    w_out,
    stale_keys,
    stale_values,
    gn2_gain,
    conv_weight,
    time_shift,
):
    row_count, col_count, channels = latent.shape
    tok_count = row_count * col_count
    peers = lax.axis_size("patch")
    x = latent.reshape(tok_count, channels)
    stats, old, *weights = norm_stats(x, stale_keys, stale_values, (w_query, w_key, w_value), peers)
    from_below = shifted(old, 1, 0, 0)
    from_above = shifted(old, -1, 0, 0)
    from_side = shifted(old, 0, 0, 1)
    stats = everyones(stats)
    queries, fresh_keys, fresh_values, fresh = project(stats, x, gn_gain, *weights)

    relayed, _ = lax.optimization_barrier((from_side, stats))
    side_below = shifted(relayed, 1, 0, 0)
    side_above = shifted(relayed, -1, 0, 0)
    beside = [shifted(queries, 0, 1, 0), shifted(queries, 0, -1, 0)]
    across = [shifted(queries, 0, 2, 0)]
    last_keys = shifted(jnp.concatenate([from_below[:tok_count], side_below[:tok_count]]), 1, 0, 0)
    last_values = shifted(jnp.concatenate([from_above[tok_count:], side_above[tok_count:]]), -1, 0, 0)

    whole = lambda block: (block, 0, block, 1)
    near = [whole(from_below), whole(from_above), whole(from_side)]
    far = [whole(side_below), whole(side_above)]
    far += [(last_keys, 0, last_values, 0), (last_keys, 1, last_values, 1)]
    own_state = attend("near_own", [queries], [whole(fresh)] + near)
    beside_state = attend("near_beside", beside, [whole(old)] + near, after=own_state[1:2], unroll=True)
    across_state = attend("near_across", across, [whole(old)] + near, after=beside_state[1:2])
    (to_across,) = attend("far_across", across, far, across_state, final=True, extra=2)
    from_across = shifted(to_across, 0, 2, 0)
    to_beside = attend("far_beside", beside, far, beside_state, final=True, after=(to_across,), weight=1, unroll=True)
    own_part, weight = attend(
        "far_own", [queries], far, own_state, final=True, after=to_beside[:1], carry=conv_weight, weight=1
    )
    parts = (
        from_across,
        shifted(to_beside[0], 0, -1, 0),
        shifted(to_beside[1], 0, 1, 0),
        own_part,
    )
    hidden, stats = merge(parts, x, w_out, peers)
    down = [(i, i + 1) for i in range(peers - 1)]
    above = lax.ppermute(hidden[tok_count - col_count :], "patch", down)
    below = lax.ppermute(hidden[:col_count], "patch", [(j, i) for i, j in down])
    result = convolve(everyones(stats), hidden, above, below, gn2_gain, weight, time_shift)
    return (result.reshape(row_count, col_count, -1), fresh_keys, fresh_values)


def solution(mesh):
    placed = (
        P(("batch", "patch"), None, None),
        P(),
        P(),
        P(),
        P(),
        P(),
        P(("batch", "patch"), None),
        P(("batch", "patch"), None),
        P(),
        P(),
        P("batch"),
    )
    return jax.shard_map(
        shards,
        mesh=mesh,
        in_specs=placed,
        out_specs=(
            P(("batch", "patch"), None, None),
            P(("batch", "patch"), None),
            P(("batch", "patch"), None),
        ),
        check_vma=False,
    )
```

profile of v0, /device:TPU:0, one launch (start us, length us, event | category | flops | bytes accessed | tf_op | source)
XLA Modules:
  0.0 121.7 jit_solution(5172797898961814188)
XLA Ops:
  0.7 3.8 %norm_stats.1 = (f32[32,128]{1,0:T(8,128)}, bf16[512,640]{1,0:T(8,128)(2,1)}, bf16[1280,640]{1,0:T(8,128)(2,1)S(1)}, bf16[1280,640]{1,0:T(8,128)(2,1)S(1)}, bf16[1280,640]{1,0:T(8,128)(2,1)S(1)}) custom-call(bf16[256,1280]{1,0:T(8,128)(2,1)} %bitcast.10, bf16[256,640]{1,0:T(8,128)(2,1)} %k_ref.1, bf16[256,640]{1,0:T(8,128)(2,1)} %v_ref.1, ...), custom_call_target="tpu_custom_call" | custom-call | flops 1310720 | bytes 655360 | tf_op jit(solution)/shard_map/norm_stats/pallas_call | solution.py:108
  4.4 3.2 %collective-permute-start.1 = (bf16[512,640]{1,0:T(8,128)(2,1)}, bf16[512,640]{1,0:T(8,128)(2,1)S(1)}, u32[]{:S(2)}, u32[]{:S(2)}) collective-permute-start(bf16[512,640]{1,0:T(8,128)(2,1)} %get-tuple-element.33.refs_2_.refs_3_.refs_1_), channel_id=1, source_target_pairs={{0,1},{1,0},{2,3},{3,2},{4,5},{5,4},{6,7},{7,6},{8,9},{9,8},{10,11... | collective-permute-start | bytes 1966088 | tf_op jit(solution)/shard_map/ppermute | solution.py:26
  7.6 1.6 %collective-permute-start.4 = (bf16[512,640]{1,0:T(8,128)(2,1)}, bf16[512,640]{1,0:T(8,128)(2,1)S(1)}, u32[]{:S(2)}, u32[]{:S(2)}) collective-permute-start(bf16[512,640]{1,0:T(8,128)(2,1)} %get-tuple-element.33.refs_2_.refs_3_.refs_1_), channel_id=1, source_target_pairs={{0,8},{1,9},{2,10},{3,11},{4,12},{5,13},{6,14},{7,15},{8,16},{9,17... | collective-permute-start | bytes 1966088 | tf_op jit(solution)/shard_map/ppermute | solution.py:26
  9.2 1.7 %collective-permute-start.6 = (bf16[512,640]{1,0:T(8,128)(2,1)}, bf16[512,640]{1,0:T(8,128)(2,1)S(1)}, u32[]{:S(2)}, u32[]{:S(2)}) collective-permute-start(bf16[512,640]{1,0:T(8,128)(2,1)} %get-tuple-element.33.refs_2_.refs_3_.refs_1_), channel_id=1, source_target_pairs={{0,24},{1,25},{2,26},{3,27},{4,28},{5,29},{6,30},{7,31},{8,0},{9,1... | collective-permute-start | bytes 1966088 | tf_op jit(solution)/shard_map/ppermute | solution.py:26
  10.9 19.2 %all_to_all.22 = f32[32,1,128]{2,1,0:T(1,128)S(1)} all-to-all(f32[32,1,128]{2,1,0:T(1,128)} %bitcast.17), channel_id=1, replica_groups=mesh['batch'=4,'patch'=32] {'patch'}, dimensions={0} | all-to-all | bytes 32768 | tf_op jit(solution)/shard_map/all_to_all | solution.py:362
  30.1 0.0 collective-permute-done.1.refs_7_.refs_8_.refs_9_
  30.1 1.8 %collective-permute-start.3 = (bf16[512,640]{1,0:T(8,128)(2,1)S(1)}, bf16[512,640]{1,0:T(8,128)(2,1)S(1)}, u32[]{:S(2)}, u32[]{:S(2)}) collective-permute-start(bf16[512,640]{1,0:T(8,128)(2,1)S(1)} %collective-permute-done.1.refs_7_.refs_8_.refs_9_), channel_id=1, source_target_pairs={{0,24},{1,25},{2,26},{3,27},{4,28},{5,29},{6,30},{7,31},{8,0},{9,1... | collective-permute-start | bytes 1966088 | tf_op jit(solution)/shard_map/ppermute | solution.py:26
  31.9 0.2 collective-permute-start.2
  32.1 2.9 %project.1 = (bf16[256,640]{1,0:T(8,128)(2,1)S(1)}, bf16[256,640]{1,0:T(8,128)(2,1)}, bf16[256,640]{1,0:T(8,128)(2,1)}, bf16[512,640]{1,0:T(8,128)(2,1)S(1)}) custom-call(f32[32,128]{1,0:T(8,128)S(1)} %bitcast.13, bf16[256,1280]{1,0:T(8,128)(2,1)S(1)} %bitcast.11, f32[1280]{0:T(1024)S(1)} %copy-done.7, bf16[1280,640]{1,0:T(8,128)(2,1)S(1)} %get-tuple-element.29.wq, ...), custom_call_target="tpu_custom_call" | custom-call | flops 1258291200 | bytes 4915200 | tf_op jit(solution)/shard_map/project/pallas_call | solution.py:139
  35.0 0.8 collective-permute-start.8
  35.9 0.0 collective-permute-done.4.refs_3_.refs_4_.refs_5_
  35.9 2.4 %collective-permute-start.9 = (bf16[256,640]{1,0:T(8,128)(2,1)S(1)}, bf16[256,640]{1,0:T(8,128)(2,1)S(1)}, u32[]{:S(2)}, u32[]{:S(2)}) collective-permute-start(bf16[256,640]{1,0:T(8,128)(2,1)S(1)} %get-tuple-element.32.refs_0_), channel_id=1, source_target_pairs={{0,6},{1,7},{2,0},{3,1},{4,2},{5,3},{6,4},{7,5},{8,14},{9,15},{10,... | collective-permute-start | bytes 983048 | tf_op jit(solution)/shard_map/ppermute | solution.py:26
  38.3 0.0 collective-permute-done.6.refs_5_.refs_6_.refs_7_
  38.3 0.2 collective-permute-start
  38.5 5.6 %near_own.1 = (f32[256,640]{1,0:T(8,128)S(1)}, f32[256,640]{1,0:T(8,128)S(1)}, f32[256,640]{1,0:T(8,128)S(1)}) custom-call(bf16[256,640]{1,0:T(8,128)(2,1)S(1)} %get-tuple-element.32.refs_0_, bf16[512,640]{1,0:T(8,128)(2,1)S(1)} %get-tuple-element.35.refs_1_.refs_2_, bf16[512,640]{1,0:T(8,128)(2,1)S(1)} %get-tuple-element.35.refs_1_.refs_2_, ...), custom_call_target="tpu_custom_call" | custom-call | flops 2684354560 | bytes 524288 | tf_op jit(solution)/shard_map/near_own/pallas_call | solution.py:255
  44.1 0.0 slice-start.1
  44.1 0.0 slice-start
  44.2 0.9 collective-permute-done.3.refs_3_.refs_4_.refs_5_
  45.1 0.0 slice-done.1
  45.1 0.1 pad_maximum_fusion.1
  45.2 3.1 %collective-permute-start.7 = (bf16[512,640]{1,0:T(8,128)(2,1)S(1)}, bf16[512,640]{1,0:T(8,128)(2,1)S(1)}, u32[]{:S(2)}, u32[]{:S(2)}) collective-permute-start(bf16[512,640]{1,0:T(8,128)(2,1)S(1)} %pad_maximum_fusion.1), channel_id=1, source_target_pairs={{0,24},{1,25},{2,26},{3,27},{4,28},{5,29},{6,30},{7,31},{8,0},{9,1... | collective-permute-start | bytes 1966088 | tf_op jit(solution)/shard_map/ppermute | solution.py:26
  48.3 0.0 collective-permute-done.2.refs_1_.refs_2_.refs_3_
  48.3 0.1 pad_maximum_fusion
  48.4 0.3 collective-permute-start.5
  48.6 2.0 %collective-permute-done.8.refs_0_ = bf16[256,640]{1,0:T(8,128)(2,1)S(1)} collective-permute-done((bf16[256,640]{1,0:T(8,128)(2,1)S(1)}, bf16[256,640]{1,0:T(8,128)(2,1)S(1)}, u32[]{:S(2)}, u32[]{:S(2)}) %collective-permute-start.8) | collective-permute-done | bytes 327712 | tf_op jit(solution)/shard_map/ppermute | solution.py:26
  50.6 0.0 collective-permute-done.9.refs_1_
  50.6 6.3 %near_beside.1 = (f32[512,640]{1,0:T(8,128)S(1)}, f32[512,640]{1,0:T(8,128)S(1)}, f32[512,640]{1,0:T(8,128)S(1)}) custom-call(bf16[256,640]{1,0:T(8,128)(2,1)S(1)} %collective-permute-done.8.refs_0_, bf16[256,640]{1,0:T(8,128)(2,1)S(1)} %collective-permute-done.9.refs_1_, bf16[512,640]{1,0:T(8,128)(2,1)S(1)} %copy-done.9, bf16[512,640]{1,0:T(8,128)(2,1)S(1)} %copy-done.9, ...), custom_call_target="tpu_custom_call" | custom-call | flops 5368709120 | bytes 524288 | tf_op jit(solution)/shard_map/near_beside/pallas_call | solution.py:255
  57.0 0.0 collective-permute-done.refs_0_
  57.0 5.6 %near_across.1 = (f32[256,640]{1,0:T(8,128)S(1)}, f32[256,640]{1,0:T(8,128)S(1)}, f32[256,640]{1,0:T(8,128)S(1)}) custom-call(bf16[256,640]{1,0:T(8,128)(2,1)S(1)} %collective-permute-done.refs_0_, bf16[512,640]{1,0:T(8,128)(2,1)S(1)} %copy-done.9, bf16[512,640]{1,0:T(8,128)(2,1)S(1)} %copy-done.9, bf16[512,640]{1,0:T(8,128)(2,1)S(1)} %copy-done.3, ...), custom_call_target="tpu_custom_call" | custom-call | flops 2684354560 | bytes 524288 | tf_op jit(solution)/shard_map/near_across/pallas_call | solution.py:255
  62.6 0.0 collective-permute-done.7.refs_6_.refs_8_.refs_7_.refs_9_
  62.6 0.5 collective-permute-done.5.refs_5_.refs_7_.refs_6_.refs_8_
  63.1 6.1 %far_across.1.refs_13_ = bf16[256,896]{1,0:T(8,128)(2,1)S(1)} custom-call(bf16[256,640]{1,0:T(8,128)(2,1)S(1)} %collective-permute-done.refs_0_, bf16[512,640]{1,0:T(8,128)(2,1)S(1)} %collective-permute-done.2.refs_1_.refs_2_.refs_3_, bf16[512,640]{1,0:T(8,128)(2,1)S(1)} %collective-permute-done.2.refs_1_.refs_2_.refs_3_, ...), custom_call_target="tpu_custom_call" | custom-call | flops 2684354560 | bytes 524288 | tf_op jit(solution)/shard_map/far_across/pallas_call | solution.py:255
  69.2 3.4 %collective-permute-start.10 = (bf16[256,896]{1,0:T(8,128)(2,1)S(1)}, bf16[256,896]{1,0:T(8,128)(2,1)S(1)}, u32[]{:S(2)}, u32[]{:S(2)}) collective-permute-start(bf16[256,896]{1,0:T(8,128)(2,1)S(1)} %far_across.1.refs_13_), channel_id=1, source_target_pairs={{0,4},{1,5},{2,6},{3,7},{4,0},{5,1},{6,2},{7,3},{8,12},{9,13},{10,... | collective-permute-start | bytes 1376264 | tf_op jit(solution)/shard_map/ppermute | solution.py:26
  72.6 7.3 %far_beside.1 = (bf16[256,768]{1,0:T(8,128)(2,1)S(1)}, bf16[256,768]{1,0:T(8,128)(2,1)S(1)}) custom-call(bf16[256,640]{1,0:T(8,128)(2,1)S(1)} %collective-permute-done.8.refs_0_, bf16[256,640]{1,0:T(8,128)(2,1)S(1)} %collective-permute-done.9.refs_1_, bf16[512,640]{1,0:T(8,128)(2,1)S(1)} %collective-permute-done.2.refs_1_.refs_2_.refs_3_, ...), custom_call_target="tpu_custom_call" | custom-call | flops 335544320 | bytes 32768 | tf_op jit(solution)/shard_map/far_beside/pallas_call | solution.py:255
  79.9 0.5 collective-permute-start.11
  80.4 1.6 %collective-permute-start.12 = (bf16[256,768]{1,0:T(8,128)(2,1)S(1)}, bf16[256,768]{1,0:T(8,128)(2,1)S(1)}, u32[]{:S(2)}, u32[]{:S(2)}) collective-permute-start(bf16[256,768]{1,0:T(8,128)(2,1)S(1)} %get-tuple-element.44), channel_id=1, source_target_pairs={{0,2},{1,3},{2,4},{3,5},{4,6},{5,7},{6,0},{7,1},{8,10},{9,11},{10,... | collective-permute-start | bytes 1179656 | tf_op jit(solution)/shard_map/ppermute | solution.py:26
  82.0 6.2 %far_own.1 = (bf16[256,768]{1,0:T(8,128)(2,1)S(1)}, bf16[9,1280,640]{2,1,0:T(8,128)(2,1)S(1)}) custom-call(bf16[256,640]{1,0:T(8,128)(2,1)S(1)} %get-tuple-element.32.refs_0_, bf16[512,640]{1,0:T(8,128)(2,1)S(1)} %collective-permute-done.2.refs_1_.refs_2_.refs_3_, bf16[512,640]{1,0:T(8,128)(2,1)S(1)} %collective-permute-done.2.refs_1_.refs_2_.refs_3_, ...), custom_call_target="tpu_custom_call" | custom-call | flops 167772160 | bytes 32768 | tf_op jit(solution)/shard_map/far_own/pallas_call | solution.py:255
  88.2 0.0 collective-permute-done.11.p1
  88.2 1.2 collective-permute-done.12.p2
  89.4 0.0 collective-permute-done.10.p0
  89.4 2.5 %merge_project.1 = (f32[256,1280]{1,0:T(8,128)S(1)}, f32[32,128]{1,0:T(8,128)S(1)}) custom-call(bf16[256,896]{1,0:T(8,128)(2,1)S(1)} %collective-permute-done.10.p0, bf16[256,768]{1,0:T(8,128)(2,1)S(1)} %collective-permute-done.11.p1, bf16[256,768]{1,0:T(8,128)(2,1)S(1)} %collective-permute-done.12.p2, bf16[256,768]{1,0:T(8,128)(2,1)S(1)} %get-tuple-element.47.p3, ...), custom_call_target="tpu_custom_call" | custom-call | flops 419430400 | bytes 1638400 | tf_op jit(solution)/shard_map/merge_project/pallas_call | solution.py:299
  91.9 0.0 copy-start.8
  91.9 4.3 %collective-permute-start.13 = (f32[64,1280]{1,0:T(8,128)S(1)}, f32[64,1280]{1,0:T(8,128)S(1)}, u32[]{:S(2)}, u32[]{:S(2)}) collective-permute-start(f32[64,1280]{1,0:T(8,128)S(1)} %get-tuple-element.54), channel_id=1, source_target_pairs={{0,1},{1,2},{2,3},{3,4},{4,5},{5,6},{6,7},{7,8},{8,9},{9,10},{10,1... | collective-permute-start | bytes 983048 | tf_op jit(solution)/shard_map/ppermute | solution.py:418
  96.3 1.3 %collective-permute-start.14 = (f32[64,1280]{1,0:T(8,128)S(1)}, f32[64,1280]{1,0:T(8,128)S(1)}, u32[]{:S(2)}, u32[]{:S(2)}) collective-permute-start(f32[64,1280]{1,0:T(8,128)S(1)} %get-tuple-element.53), channel_id=1, source_target_pairs={{1,0},{2,1},{3,2},{4,3},{5,4},{6,5},{7,6},{8,7},{9,8},{10,9},{11,1... | collective-permute-start | bytes 983048 | tf_op jit(solution)/shard_map/ppermute | solution.py:419
  97.6 17.7 %all_to_all.23 = f32[32,1,128]{2,1,0:T(1,128)S(1)} all-to-all(f32[32,1,128]{2,1,0:T(1,128)S(1)} %bitcast.15), channel_id=1, replica_groups=mesh['batch'=4,'patch'=32] {'patch'}, dimensions={0} | all-to-all | bytes 32768 | tf_op jit(solution)/shard_map/all_to_all | solution.py:362
  115.3 0.0 collective-permute-done.13.above_ref
  115.3 0.0 collective-permute-done.14.below_ref
  115.3 6.5 %norm_convolve.1 = bf16[256,640]{1,0:T(8,128)(2,1)} custom-call(f32[32,128]{1,0:T(8,128)S(1)} %bitcast.14, f32[256,1280]{1,0:T(8,128)S(1)} %get-tuple-element.49.hidden_ref, f32[64,1280]{1,0:T(8,128)S(1)} %collective-permute-done.13.above_ref, f32[64,1280]{1,0:T(8,128)S(1)} %collective-permute-done.14.below_ref, f32[1280]{0:T(1024)S(1)} %copy-done.6, ...), custom_call_target="tpu_custom_call" | custom-call | flops 3774873600 | bytes 14745600 | tf_op jit(solution)/shard_map/norm_convolve/pallas_call | solution.py:347
  (23 shorter events, 0.1 us)
Async XLA Ops:
  0.6 31.5 %copy-start = (bf16[4,64,1280]{2,1,0:T(8,128)(2,1)S(1)}, bf16[4,64,1280]{2,1,0:T(8,128)(2,1)}, u32[]{:S(2)}) copy-start(bf16[4,64,1280]{2,1,0:T(8,128)(2,1)} %param.11) | copy-start | bytes 1966084
  0.6 31.5 %copy-start.7 = (f32[1280]{0:T(1024)S(1)}, f32[1280]{0:T(1024)}, u32[]{:S(2)}) copy-start(f32[1280]{0:T(1024)} %gain_ref.2) | copy-start | bytes 15364
  4.4 25.7 %collective-permute-start.1 = (bf16[512,640]{1,0:T(8,128)(2,1)}, bf16[512,640]{1,0:T(8,128)(2,1)S(1)}, u32[]{:S(2)}, u32[]{:S(2)}) collective-permute-start(bf16[512,640]{1,0:T(8,128)(2,1)} %get-tuple-element.33.refs_2_.refs_3_.refs_1_), channel_id=1, source_target_pairs={{0,1},{1,0},{2,3},{3,2},{4,5},{5,4},{6,7},{7,6},{8,9},{9,8},{10,11... | collective-permute-start | bytes 1966088 | tf_op jit(solution)/shard_map/ppermute | solution.py:26
  7.6 28.3 %collective-permute-start.4 = (bf16[512,640]{1,0:T(8,128)(2,1)}, bf16[512,640]{1,0:T(8,128)(2,1)S(1)}, u32[]{:S(2)}, u32[]{:S(2)}) collective-permute-start(bf16[512,640]{1,0:T(8,128)(2,1)} %get-tuple-element.33.refs_2_.refs_3_.refs_1_), channel_id=1, source_target_pairs={{0,8},{1,9},{2,10},{3,11},{4,12},{5,13},{6,14},{7,15},{8,16},{9,17... | collective-permute-start | bytes 1966088 | tf_op jit(solution)/shard_map/ppermute | solution.py:26
  9.2 29.1 %collective-permute-start.6 = (bf16[512,640]{1,0:T(8,128)(2,1)}, bf16[512,640]{1,0:T(8,128)(2,1)S(1)}, u32[]{:S(2)}, u32[]{:S(2)}) collective-permute-start(bf16[512,640]{1,0:T(8,128)(2,1)} %get-tuple-element.33.refs_2_.refs_3_.refs_1_), channel_id=1, source_target_pairs={{0,24},{1,25},{2,26},{3,27},{4,28},{5,29},{6,30},{7,31},{8,0},{9,1... | collective-permute-start | bytes 1966088 | tf_op jit(solution)/shard_map/ppermute | solution.py:26
  30.1 14.9 %collective-permute-start.3 = (bf16[512,640]{1,0:T(8,128)(2,1)S(1)}, bf16[512,640]{1,0:T(8,128)(2,1)S(1)}, u32[]{:S(2)}, u32[]{:S(2)}) collective-permute-start(bf16[512,640]{1,0:T(8,128)(2,1)S(1)} %collective-permute-done.1.refs_7_.refs_8_.refs_9_), channel_id=1, source_target_pairs={{0,24},{1,25},{2,26},{3,27},{4,28},{5,29},{6,30},{7,31},{8,0},{9,1... | collective-permute-start | bytes 1966088 | tf_op jit(solution)/shard_map/ppermute | solution.py:26
  31.9 16.4 %collective-permute-start.2 = (bf16[512,640]{1,0:T(8,128)(2,1)S(1)}, bf16[512,640]{1,0:T(8,128)(2,1)S(1)}, u32[]{:S(2)}, u32[]{:S(2)}) collective-permute-start(bf16[512,640]{1,0:T(8,128)(2,1)S(1)} %collective-permute-done.1.refs_7_.refs_8_.refs_9_), channel_id=1, source_target_pairs={{0,8},{1,9},{2,10},{3,11},{4,12},{5,13},{6,14},{7,15},{8,16},{9,17... | collective-permute-start | bytes 1966088 | tf_op jit(solution)/shard_map/ppermute | solution.py:26
  35.0 15.6 %collective-permute-start.8 = (bf16[256,640]{1,0:T(8,128)(2,1)S(1)}, bf16[256,640]{1,0:T(8,128)(2,1)S(1)}, u32[]{:S(2)}, u32[]{:S(2)}) collective-permute-start(bf16[256,640]{1,0:T(8,128)(2,1)S(1)} %get-tuple-element.32.refs_0_), channel_id=1, source_target_pairs={{0,2},{1,3},{2,4},{3,5},{4,6},{5,7},{6,0},{7,1},{8,10},{9,11},{10,... | collective-permute-start | bytes 983048 | tf_op jit(solution)/shard_map/ppermute | solution.py:26
  35.9 8.2 %copy-start.2 = (bf16[512,640]{1,0:T(8,128)(2,1)}, bf16[512,640]{1,0:T(8,128)(2,1)S(1)}, u32[]{:S(2)}) copy-start(bf16[512,640]{1,0:T(8,128)(2,1)S(1)} %collective-permute-done.4.refs_3_.refs_4_.refs_5_) | copy-start | bytes 1966084
  35.9 14.7 %collective-permute-start.9 = (bf16[256,640]{1,0:T(8,128)(2,1)S(1)}, bf16[256,640]{1,0:T(8,128)(2,1)S(1)}, u32[]{:S(2)}, u32[]{:S(2)}) collective-permute-start(bf16[256,640]{1,0:T(8,128)(2,1)S(1)} %get-tuple-element.32.refs_0_), channel_id=1, source_target_pairs={{0,6},{1,7},{2,0},{3,1},{4,2},{5,3},{6,4},{7,5},{8,14},{9,15},{10,... | collective-permute-start | bytes 983048 | tf_op jit(solution)/shard_map/ppermute | solution.py:26
  38.3 5.8 %copy-start.4 = (bf16[512,640]{1,0:T(8,128)(2,1)}, bf16[512,640]{1,0:T(8,128)(2,1)S(1)}, u32[]{:S(2)}) copy-start(bf16[512,640]{1,0:T(8,128)(2,1)S(1)} %collective-permute-done.6.refs_5_.refs_6_.refs_7_) | copy-start | bytes 1966084
  38.3 18.7 %collective-permute-start = (bf16[256,640]{1,0:T(8,128)(2,1)S(1)}, bf16[256,640]{1,0:T(8,128)(2,1)S(1)}, u32[]{:S(2)}, u32[]{:S(2)}) collective-permute-start(bf16[256,640]{1,0:T(8,128)(2,1)S(1)} %get-tuple-element.32.refs_0_), channel_id=1, source_target_pairs={{0,4},{1,5},{2,6},{3,7},{4,0},{5,1},{6,2},{7,3},{8,12},{9,13},{10,... | collective-permute-start | bytes 983048 | tf_op jit(solution)/shard_map/ppermute | solution.py:26
  44.1 1.0 slice-start.1
  44.1 4.2 %slice-start = ((bf16[512,640]{1,0:T(8,128)(2,1)}), bf16[256,640]{1,0:T(8,128)(2,1)S(1)}, s32[]{:S(2)}) async-start(bf16[512,640]{1,0:T(8,128)(2,1)} %copy-done.2), calls=%async_computation.2 | async-start | bytes 655360 | tf_op jit(solution)/shard_map/slice | solution.py:394
  45.2 5.5 %copy-start.3 = (bf16[512,640]{1,0:T(8,128)(2,1)S(1)}, bf16[512,640]{1,0:T(8,128)(2,1)}, u32[]{:S(2)}) copy-start(bf16[512,640]{1,0:T(8,128)(2,1)} %copy-done.2) | copy-start | bytes 1966084
  45.2 5.5 %copy-start.5 = (bf16[512,640]{1,0:T(8,128)(2,1)S(1)}, bf16[512,640]{1,0:T(8,128)(2,1)}, u32[]{:S(2)}) copy-start(bf16[512,640]{1,0:T(8,128)(2,1)} %copy-done.4) | copy-start | bytes 1966084
  45.2 5.5 %copy-start.9 = (bf16[512,640]{1,0:T(8,128)(2,1)S(1)}, bf16[512,640]{1,0:T(8,128)(2,1)}, u32[]{:S(2)}) copy-start(bf16[512,640]{1,0:T(8,128)(2,1)} %get-tuple-element.33.refs_2_.refs_3_.refs_1_) | copy-start | bytes 1966084
  45.2 17.4 %collective-permute-start.7 = (bf16[512,640]{1,0:T(8,128)(2,1)S(1)}, bf16[512,640]{1,0:T(8,128)(2,1)S(1)}, u32[]{:S(2)}, u32[]{:S(2)}) collective-permute-start(bf16[512,640]{1,0:T(8,128)(2,1)S(1)} %pad_maximum_fusion.1), channel_id=1, source_target_pairs={{0,24},{1,25},{2,26},{3,27},{4,28},{5,29},{6,30},{7,31},{8,0},{9,1... | collective-permute-start | bytes 1966088 | tf_op jit(solution)/shard_map/ppermute | solution.py:26
  48.4 14.7 %collective-permute-start.5 = (bf16[512,640]{1,0:T(8,128)(2,1)S(1)}, bf16[512,640]{1,0:T(8,128)(2,1)S(1)}, u32[]{:S(2)}, u32[]{:S(2)}) collective-permute-start(bf16[512,640]{1,0:T(8,128)(2,1)S(1)} %pad_maximum_fusion), channel_id=1, source_target_pairs={{0,8},{1,9},{2,10},{3,11},{4,12},{5,13},{6,14},{7,15},{8,16},{9,17... | collective-permute-start | bytes 1966088 | tf_op jit(solution)/shard_map/ppermute | solution.py:26
  69.2 20.2 %collective-permute-start.10 = (bf16[256,896]{1,0:T(8,128)(2,1)S(1)}, bf16[256,896]{1,0:T(8,128)(2,1)S(1)}, u32[]{:S(2)}, u32[]{:S(2)}) collective-permute-start(bf16[256,896]{1,0:T(8,128)(2,1)S(1)} %far_across.1.refs_13_), channel_id=1, source_target_pairs={{0,4},{1,5},{2,6},{3,7},{4,0},{5,1},{6,2},{7,3},{8,12},{9,13},{10,... | collective-permute-start | bytes 1376264 | tf_op jit(solution)/shard_map/ppermute | solution.py:26
  79.9 8.3 %collective-permute-start.11 = (bf16[256,768]{1,0:T(8,128)(2,1)S(1)}, bf16[256,768]{1,0:T(8,128)(2,1)S(1)}, u32[]{:S(2)}, u32[]{:S(2)}) collective-permute-start(bf16[256,768]{1,0:T(8,128)(2,1)S(1)} %get-tuple-element.43.refs_12_), channel_id=1, source_target_pairs={{0,6},{1,7},{2,0},{3,1},{4,2},{5,3},{6,4},{7,5},{8,14},{9,15},{10,... | collective-permute-start | bytes 1179656 | tf_op jit(solution)/shard_map/ppermute | solution.py:26
  80.4 9.0 %collective-permute-start.12 = (bf16[256,768]{1,0:T(8,128)(2,1)S(1)}, bf16[256,768]{1,0:T(8,128)(2,1)S(1)}, u32[]{:S(2)}, u32[]{:S(2)}) collective-permute-start(bf16[256,768]{1,0:T(8,128)(2,1)S(1)} %get-tuple-element.44), channel_id=1, source_target_pairs={{0,2},{1,3},{2,4},{3,5},{4,6},{5,7},{6,0},{7,1},{8,10},{9,11},{10,... | collective-permute-start | bytes 1179656 | tf_op jit(solution)/shard_map/ppermute | solution.py:26
  82.0 7.4 %copy-start.1 = (bf16[640,1280]{1,0:T(8,128)(2,1)S(1)}, bf16[640,1280]{1,0:T(8,128)(2,1)}, u32[]{:S(2)}) copy-start(bf16[640,1280]{1,0:T(8,128)(2,1)} %w_ref.1) | copy-start | bytes 4915204
  91.8 23.4 %copy-start.6 = (f32[1280]{0:T(1024)S(1)}, f32[1280]{0:T(1024)}, u32[]{:S(2)}) copy-start(f32[1280]{0:T(1024)} %gain_ref.3) | copy-start | bytes 15364
  91.9 23.4 %copy-start.8 = (f32[640]{0:T(1024)S(1)}, f32[640]{0:T(1024)}, u32[]{:S(2)}) copy-start(f32[640]{0:T(1024)} %shift_ref.1) | copy-start | bytes 7684
  91.9 23.3 %collective-permute-start.13 = (f32[64,1280]{1,0:T(8,128)S(1)}, f32[64,1280]{1,0:T(8,128)S(1)}, u32[]{:S(2)}, u32[]{:S(2)}) collective-permute-start(f32[64,1280]{1,0:T(8,128)S(1)} %get-tuple-element.54), channel_id=1, source_target_pairs={{0,1},{1,2},{2,3},{3,4},{4,5},{5,6},{6,7},{7,8},{8,9},{9,10},{10,1... | collective-permute-start | bytes 983048 | tf_op jit(solution)/shard_map/ppermute | solution.py:418
  96.3 19.0 %collective-permute-start.14 = (f32[64,1280]{1,0:T(8,128)S(1)}, f32[64,1280]{1,0:T(8,128)S(1)}, u32[]{:S(2)}, u32[]{:S(2)}) collective-permute-start(f32[64,1280]{1,0:T(8,128)S(1)} %get-tuple-element.53), channel_id=1, source_target_pairs={{1,0},{2,1},{3,2},{4,3},{5,4},{6,5},{7,6},{8,7},{9,8},{10,9},{11,1... | collective-permute-start | bytes 983048 | tf_op jit(solution)/shard_map/ppermute | solution.py:419
where the time goes:
time: 122 us
  Pallas kernels  52.7 us (43%)
  blocking collectives  36.9 us (30%)
  starting transfers between devices  26.3 us (22%)
  waiting for transfers between devices  4.58 us (4%)
    pallas_call x6, Pallas kernels, attend(): pl.pallas_call(functools.partial(attend_kernel, plan, bool(state), final,...  37.1 us
    all_to_all x2, blocking collectives, everyones(): return lax.all_to_all(stats, 'patch', 0, 0, tiled=True)  36.9 us
    ppermute x13, starting transfers between devices, shifted(): return lax.ppermute(x, 'patch', pairs)  20.7 us
    pallas_call x1, Pallas kernels, convolve(): pl.pallas_call(conv_kernel, in_specs=[VMEM] * 7, out_specs=VMEM, out_shap...  6.46 us
    ppermute x13, waiting for transfers between devices, shifted(): return lax.ppermute(x, 'patch', pairs)  4.57 us
    ppermute x1, starting transfers between devices, shards(): above = lax.ppermute(hidden[tok_count - col_count:], 'patch', down)  4.34 us
    pallas_call x1, Pallas kernels, norm_stats(): pl.pallas_call(stats_kernel, in_specs=[HBM] * 6, out_specs=[VMEM] * 5, ou...  3.77 us
    pallas_call x1, Pallas kernels, project(): pl.pallas_call(project_kernel, in_specs=[VMEM] * 6, out_specs=[VMEM] * 4,...  2.92 us
  transfers between devices with their start and end apart: 15, of which 4 were waited for; matrix products, arithmetic and copies ran while one was open for 0% of the time, Pallas kernels for 28%

commit v1 on v0

--- a/solution.py
+++ b/solution.py
@@ -47,14 +47,22 @@
     )
 
 
-def local_stats(x, peers):
+def group_matrices(channels):
+    return (
+        members_of(channels, True, 0),
+        members_of(channels, False, 0),
+        members_of(channels, True, GROUPS),
+    )
+
+
+def local_stats(x, peers, matrices):
     rows, channels = x.shape
     count = rows * (channels // GROUPS)
     total = jnp.sum(x, axis=0, keepdims=True)
-    mean = exact_dot(total, members_of(channels, True, 0)) / count
-    center = exact_dot(mean, members_of(channels, False, 0))
+    mean = exact_dot(total, matrices[0]) / count
+    center = exact_dot(mean, matrices[1])
     squares = jnp.sum(jnp.square(x - center), axis=0, keepdims=True)
-    spread = exact_dot(squares, members_of(channels, True, GROUPS))
+    spread = exact_dot(squares, matrices[2])
     return jnp.broadcast_to(mean + spread, (peers, LANES))
 
 
@@ -96,9 +104,10 @@
         copies += halves(src, dst, sems, 4 + 2 * i)
     for copy in copies:
         copy.start()
+    matrices = group_matrices(x_ref.shape[1])
     for copy in copies[:2]:
         copy.wait()
-    out_ref[...] = local_stats(held[...].astype(F32), out_ref.shape[0])
+    out_ref[...] = local_stats(held[...].astype(F32), out_ref.shape[0], matrices)
     for copy in copies[2:]:
         copy.wait()
 
@@ -152,21 +161,17 @@
     )(stats, x, gain, wq, wk, wv)
 
 
-def attend_pair(queries, keys, values):
-    rows = queries.shape[0]
-    first = lax.broadcasted_iota(jnp.int32, (rows, LANES), 1) < HEAD
-    scaled = queries * BF(0.125)
-    none = jnp.zeros_like(scaled)
-    found = []
-    for mine in (jnp.where(first, scaled, none), jnp.where(first, none, scaled)):
-        scores = lax.dot_general(
-            mine, keys, (((1,), (1,)), ((), ())), preferred_element_type=F32
-        )
-        top = jnp.max(scores, axis=1, keepdims=True)
-        weights = jnp.exp(scores - top).astype(BF)
-        both = jnp.dot(weights, values, preferred_element_type=F32)
-        found.append((both[:, :LANES], jnp.broadcast_to(top, (rows, LANES)), both[:, LANES:]))
-    return first, found
+def scores_of(queries, keys, second):
+    lane = lax.broadcasted_iota(jnp.int32, queries.shape, 1)
+    mine = jnp.where((lane >= HEAD) if second else (lane < HEAD), queries * BF(0.125), BF(0))
+    return lax.dot_general(mine, keys, (((1,), (1,)), ((), ())), preferred_element_type=F32)
+
+
+def weigh(scores, values):
+    top = jnp.max(scores, axis=1, keepdims=True)
+    weights = jnp.exp(scores - top).astype(BF)
+    both = jnp.dot(weights, values, preferred_element_type=F32)
+    return both[:, :LANES], jnp.broadcast_to(top, (scores.shape[0], LANES)), both[:, LANES:]
 
 
 def attend_kernel(plan, start, final, waits, carry, unroll, *refs):
@@ -179,8 +184,10 @@
     brought = take(1 if carry else 0)
     outs = take(count if final else 3)
     copies = []
+    (kept,) = take(1) if carry else (None,)
+    (scores,) = take(1)
     if carry:
-        (kept,), (sems,) = take(1), take(1)
+        (sems,) = take(1)
         copies = [
             pltpu.make_async_copy(brought[0].at[i], kept.at[i], sems.at[i]) for i in range(kept.shape[0])
         ]
@@ -193,16 +200,30 @@
         for o_ref in outs:
             o_ref[:, width:] = jnp.zeros((rows, o_ref.shape[1] - width), BF)
 
-    def pair(j, carried):
-        cols = pl.ds(pl.multiple_of(j * LANES, LANES), LANES)
-        keys, values = [], []
-        for i, (key_row, value_row) in enumerate(rows_of):
-            keys.append(sources[2 * i][key_row * rows : (key_row + 1) * rows, cols])
-            value = sources[2 * i + 1][value_row * rows : (value_row + 1) * rows, cols]
-            values.append(jnp.concatenate([value, ones], axis=1))
-        keys, values = jnp.concatenate(keys, axis=0), jnp.concatenate(values, axis=0)
+    pairs = width // LANES
+    lanes_of = lambda j: pl.ds(pl.multiple_of(j * LANES, LANES), LANES)
+    piece = lambda ref, row, cols: ref[row * rows : (row + 1) * rows, cols]
+
+    def keys_of(cols):
+        return jnp.concatenate([piece(sources[2 * i], r, cols) for i, (r, _) in enumerate(rows_of)])
+
+    def values_of(cols):
+        found = [piece(sources[2 * i + 1], r, cols) for i, (_, r) in enumerate(rows_of)]
+        return jnp.concatenate([jnp.concatenate([v, ones], axis=1) for v in found])
+
+    def step(j, following):
+        cols = lanes_of(j)
+        values = values_of(cols)
+        if following:
+            later = lanes_of(j + 1)
+            keys = keys_of(later)
         for band, q_ref in enumerate(queries):
-            first, found = attend_pair(q_ref[:, cols], keys, values)
+            found = []
+            for h in range(2):
+                found.append(weigh(scores[2 * band + h], values))
+                if following:
+                    scores[2 * band + h] = scores_of(q_ref[:, later], keys, h)
+            first = lane < HEAD
             at = slice(band * rows, (band + 1) * rows)
             summed, top, total = (jnp.where(first, found[0][n], found[1][n]) for n in range(3))
             if state is not None:
@@ -223,14 +244,23 @@
             extra = outs[band][:, width : width + LANES]
             for h in range(2):
                 rest = row_level[h]
-                for piece in range(3):
+                for cut in range(3):
                     part = rest.astype(BF)
                     rest = rest - part.astype(F32)
-                    extra = jnp.where(lane == 2 * j + h + 10 * piece, part, extra)
+                    extra = jnp.where(lane == 2 * j + h + 10 * cut, part, extra)
             outs[band][:, width : width + LANES] = extra
+
+    start_keys = keys_of(slice(0, LANES))
+    for band, q_ref in enumerate(queries):
+        for h in range(2):
+            scores[2 * band + h] = scores_of(q_ref[:, 0:LANES], start_keys, h)
+
+    def loop_step(j, carried):
+        step(j, True)
         return carried
 
-    lax.fori_loop(0, width // LANES, pair, 0, unroll=unroll)
+    lax.fori_loop(0, pairs - 1, loop_step, 0, unroll=unroll)
+    step(pairs - 1, False)
     for copy in copies:
         copy.wait()
 
@@ -246,7 +276,8 @@
         out_shape = [jax.ShapeDtypeStruct((rows, width + extra * LANES), BF)] * count
     else:
         out_shape = [jax.ShapeDtypeStruct((count * rows, width), F32)] * 3
-    scratch, carried = [], []
+    scratch = [pltpu.VMEM((2 * count, rows, len(blocks) * rows), F32)]
+    carried = []
     if carry is not None:
         out_shape.append(pltpu.VMEM(carry.shape, carry.dtype))
         scratch.append(pltpu.SemaphoreType.DMA((carry.shape[0],)))
@@ -291,7 +322,7 @@
     attended = (summed / total).astype(BF)
     hidden = x_ref[...].astype(F32) + jnp.dot(attended, w_ref[...], preferred_element_type=F32)
     hidden_ref[...] = hidden
-    stats_ref[...] = local_stats(hidden, stats_ref.shape[0])
+    stats_ref[...] = local_stats(hidden, stats_ref.shape[0], group_matrices(hidden.shape[1]))
 
 
 def merge(parts, x, w_out, peers):
@@ -317,14 +348,14 @@
     cols = above_ref.shape[0]
     width = out_ref.shape[1]
     center, scale = combined(stats_ref[...], channels, rows * (channels // GROUPS))
-    gain = gain_ref[...].reshape(1, channels)
+    scale = 0.5 * scale * gain_ref[...].reshape(1, channels)
     col = lax.broadcasted_iota(jnp.int32, (cols, channels), 0)
     pieces = [(above_ref, 0, own != 0)]
     pieces += [(hidden_ref, i, None) for i in range(rows // cols)]
     pieces += [(below_ref, 0, own != last)]
     for place, (ref, part, kept) in enumerate(pieces):
-        v = (ref[part * cols : (part + 1) * cols, :] - center) * scale * gain
-        v = v / (1.0 + jnp.exp(-v))
+        half = (ref[part * cols : (part + 1) * cols, :] - center) * scale
+        v = half * jnp.tanh(half) + half
         if kept is not None:
             v = jnp.where(kept, v, 0.0)
         to = slice(place * cols, (place + 1) * cols)
@@ -399,9 +430,9 @@
     far = [whole(side_below), whole(side_above)]
     far += [(last_keys, 0, last_values, 0), (last_keys, 1, last_values, 1)]
     own_state = attend("near_own", [queries], [whole(fresh)] + near)
-    beside_state = attend("near_beside", beside, [whole(old)] + near, after=own_state[1:2], unroll=True)
+    beside_state = attend("near_beside", beside, [whole(old)] + near, after=own_state[1:2])
     across_state = attend("near_across", across, [whole(old)] + near, after=beside_state[1:2])
-    (to_across,) = attend("far_across", across, far, across_state, final=True, extra=2)
+    (to_across,) = attend("far_across", across, far, across_state, final=True, extra=2, unroll=True)
     from_across = shifted(to_across, 0, 2, 0)
     to_beside = attend("far_beside", beside, far, beside_state, final=True, after=(to_across,), weight=1, unroll=True)
     own_part, weight = attend(

time: 122 us -> 119 us (0.975)
  Pallas kernels: 52.7 us -> 47.6 us
  waiting for transfers between devices: 4.58 us -> 8.71 us
  starting transfers between devices: 26.3 us -> 24.8 us
    pallas_call x6, Pallas kernels: 37.1 us -> 32.3 us  [attend(): pl.pallas_call(functools.partial(attend_kernel, plan, bool(state), final,...]
    ppermute x13, waiting for transfers between devices: 4.57 us -> 8.7 us  [shifted(): return lax.ppermute(x, 'patch', pairs)]
    ppermute x13, starting transfers between devices: 20.7 us -> 19.1 us  [shifted(): return lax.ppermute(x, 'patch', pairs)]
  transfers between devices with their start and end apart: 15 -> 15, of which waited for: 4 -> 5; matrix products, arithmetic and copies ran while one was open for 0% -> 0% of each run, Pallas kernels for 28% -> 26%
where the time goes in v1:
time: 119 us
  Pallas kernels  47.6 us (40%)
  blocking collectives  36.5 us (31%)
  starting transfers between devices  24.8 us (21%)
  waiting for transfers between devices  8.71 us (7%)
    all_to_all x2, blocking collectives, everyones(): return lax.all_to_all(stats, 'patch', 0, 0, tiled=True)  36.5 us
    pallas_call x6, Pallas kernels, attend(): pl.pallas_call(functools.partial(attend_kernel, plan, bool(state), final,...  32.3 us
    ppermute x13, starting transfers between devices, shifted(): return lax.ppermute(x, 'patch', pairs)  19.1 us
    ppermute x13, waiting for transfers between devices, shifted(): return lax.ppermute(x, 'patch', pairs)  8.7 us
    pallas_call x1, Pallas kernels, convolve(): pl.pallas_call(conv_kernel, in_specs=[VMEM] * 7, out_specs=VMEM, out_shap...  6.21 us
    ppermute x1, starting transfers between devices, shards(): above = lax.ppermute(hidden[tok_count - col_count:], 'patch', down)  4.33 us
    pallas_call x1, Pallas kernels, norm_stats(): pl.pallas_call(stats_kernel, in_specs=[HBM] * 6, out_specs=[VMEM] * 5, ou...  3.77 us
    pallas_call x1, Pallas kernels, project(): pl.pallas_call(project_kernel, in_specs=[VMEM] * 6, out_specs=[VMEM] * 4,...  2.92 us
  transfers between devices with their start and end apart: 15, of which 5 were waited for; matrix products, arithmetic and copies ran while one was open for 0% of the time, Pallas kernels for 26%

profile of v1, /device:TPU:0, one launch (start us, length us, event | category | flops | bytes accessed | tf_op | source)
XLA Modules:
  0.0 118.8 jit_solution(17426270151039569580)
XLA Ops:
  0.7 3.8 %norm_stats.1 = (f32[32,128]{1,0:T(8,128)}, bf16[512,640]{1,0:T(8,128)(2,1)}, bf16[1280,640]{1,0:T(8,128)(2,1)S(1)}, bf16[1280,640]{1,0:T(8,128)(2,1)S(1)}, bf16[1280,640]{1,0:T(8,128)(2,1)S(1)}) custom-call(bf16[256,1280]{1,0:T(8,128)(2,1)} %bitcast.10, bf16[256,640]{1,0:T(8,128)(2,1)} %k_ref.1, bf16[256,640]{1,0:T(8,128)(2,1)} %v_ref.1, ...), custom_call_target="tpu_custom_call" | custom-call | flops 1310720 | bytes 655360 | tf_op jit(solution)/shard_map/norm_stats/pallas_call | solution.py:117
  4.4 3.2 %collective-permute-start.1 = (bf16[512,640]{1,0:T(8,128)(2,1)}, bf16[512,640]{1,0:T(8,128)(2,1)S(1)}, u32[]{:S(2)}, u32[]{:S(2)}) collective-permute-start(bf16[512,640]{1,0:T(8,128)(2,1)} %get-tuple-element.33.refs_2_.refs_3_.refs_1_), channel_id=1, source_target_pairs={{0,1},{1,0},{2,3},{3,2},{4,5},{5,4},{6,7},{7,6},{8,9},{9,8},{10,11... | collective-permute-start | bytes 1966088 | tf_op jit(solution)/shard_map/ppermute | solution.py:26
  7.6 1.6 %collective-permute-start.4 = (bf16[512,640]{1,0:T(8,128)(2,1)}, bf16[512,640]{1,0:T(8,128)(2,1)S(1)}, u32[]{:S(2)}, u32[]{:S(2)}) collective-permute-start(bf16[512,640]{1,0:T(8,128)(2,1)} %get-tuple-element.33.refs_2_.refs_3_.refs_1_), channel_id=1, source_target_pairs={{0,8},{1,9},{2,10},{3,11},{4,12},{5,13},{6,14},{7,15},{8,16},{9,17... | collective-permute-start | bytes 1966088 | tf_op jit(solution)/shard_map/ppermute | solution.py:26
  9.2 1.7 %collective-permute-start.6 = (bf16[512,640]{1,0:T(8,128)(2,1)}, bf16[512,640]{1,0:T(8,128)(2,1)S(1)}, u32[]{:S(2)}, u32[]{:S(2)}) collective-permute-start(bf16[512,640]{1,0:T(8,128)(2,1)} %get-tuple-element.33.refs_2_.refs_3_.refs_1_), channel_id=1, source_target_pairs={{0,24},{1,25},{2,26},{3,27},{4,28},{5,29},{6,30},{7,31},{8,0},{9,1... | collective-permute-start | bytes 1966088 | tf_op jit(solution)/shard_map/ppermute | solution.py:26
  10.9 19.2 %all_to_all.22 = f32[32,1,128]{2,1,0:T(1,128)S(1)} all-to-all(f32[32,1,128]{2,1,0:T(1,128)} %bitcast.17), channel_id=1, replica_groups=mesh['batch'=4,'patch'=32] {'patch'}, dimensions={0} | all-to-all | bytes 32768 | tf_op jit(solution)/shard_map/all_to_all | solution.py:393
  30.1 0.0 collective-permute-done.1.refs_7_.refs_8_.refs_9_
  30.1 1.8 %collective-permute-start.3 = (bf16[512,640]{1,0:T(8,128)(2,1)S(1)}, bf16[512,640]{1,0:T(8,128)(2,1)S(1)}, u32[]{:S(2)}, u32[]{:S(2)}) collective-permute-start(bf16[512,640]{1,0:T(8,128)(2,1)S(1)} %collective-permute-done.1.refs_7_.refs_8_.refs_9_), channel_id=1, source_target_pairs={{0,24},{1,25},{2,26},{3,27},{4,28},{5,29},{6,30},{7,31},{8,0},{9,1... | collective-permute-start | bytes 1966088 | tf_op jit(solution)/shard_map/ppermute | solution.py:26
  31.9 0.2 collective-permute-start.2
  32.1 0.0 copy-done
  32.1 2.9 %project.1 = (bf16[256,640]{1,0:T(8,128)(2,1)S(1)}, bf16[256,640]{1,0:T(8,128)(2,1)}, bf16[256,640]{1,0:T(8,128)(2,1)}, bf16[512,640]{1,0:T(8,128)(2,1)S(1)}) custom-call(f32[32,128]{1,0:T(8,128)S(1)} %bitcast.13, bf16[256,1280]{1,0:T(8,128)(2,1)S(1)} %bitcast.11, f32[1280]{0:T(1024)S(1)} %copy-done.7, bf16[1280,640]{1,0:T(8,128)(2,1)S(1)} %get-tuple-element.29.wq, ...), custom_call_target="tpu_custom_call" | custom-call | flops 1258291200 | bytes 4915200 | tf_op jit(solution)/shard_map/project/pallas_call | solution.py:148
  35.0 0.8 collective-permute-start.8
  35.9 0.0 collective-permute-done.4.refs_3_.refs_4_.refs_5_
  35.9 2.4 %collective-permute-start.9 = (bf16[256,640]{1,0:T(8,128)(2,1)S(1)}, bf16[256,640]{1,0:T(8,128)(2,1)S(1)}, u32[]{:S(2)}, u32[]{:S(2)}) collective-permute-start(bf16[256,640]{1,0:T(8,128)(2,1)S(1)} %get-tuple-element.32.refs_0_), channel_id=1, source_target_pairs={{0,6},{1,7},{2,0},{3,1},{4,2},{5,3},{6,4},{7,5},{8,14},{9,15},{10,... | collective-permute-start | bytes 983048 | tf_op jit(solution)/shard_map/ppermute | solution.py:26
  38.3 0.0 collective-permute-done.6.refs_5_.refs_6_.refs_7_
  38.3 0.2 collective-permute-start
  38.5 4.2 %near_own.1 = (f32[256,640]{1,0:T(8,128)S(1)}, f32[256,640]{1,0:T(8,128)S(1)}, f32[256,640]{1,0:T(8,128)S(1)}) custom-call(bf16[256,640]{1,0:T(8,128)(2,1)S(1)} %get-tuple-element.32.refs_0_, bf16[512,640]{1,0:T(8,128)(2,1)S(1)} %get-tuple-element.35.refs_1_.refs_2_, bf16[512,640]{1,0:T(8,128)(2,1)S(1)} %get-tuple-element.35.refs_1_.refs_2_, ...), custom_call_target="tpu_custom_call" | custom-call | flops 2684354560 | bytes 524288 | tf_op jit(solution)/shard_map/near_own/pallas_call | solution.py:286
  42.8 0.0 slice-start.1
  42.8 0.0 slice-start
  42.8 2.2 %collective-permute-done.3.refs_3_.refs_4_.refs_5_ = bf16[512,640]{1,0:T(8,128)(2,1)S(1)} collective-permute-done((bf16[512,640]{1,0:T(8,128)(2,1)S(1)}, bf16[512,640]{1,0:T(8,128)(2,1)S(1)}, u32[]{:S(2)}, u32[]{:S(2)}) %collective-permute-start.3) | collective-permute-done | bytes 655392 | tf_op jit(solution)/shard_map/ppermute | solution.py:26
  45.1 0.1 pad_maximum_fusion.1
  45.2 2.9 %collective-permute-start.7 = (bf16[512,640]{1,0:T(8,128)(2,1)S(1)}, bf16[512,640]{1,0:T(8,128)(2,1)S(1)}, u32[]{:S(2)}, u32[]{:S(2)}) collective-permute-start(bf16[512,640]{1,0:T(8,128)(2,1)S(1)} %pad_maximum_fusion.1), channel_id=1, source_target_pairs={{0,24},{1,25},{2,26},{3,27},{4,28},{5,29},{6,30},{7,31},{8,0},{9,1... | collective-permute-start | bytes 1966088 | tf_op jit(solution)/shard_map/ppermute | solution.py:26
  48.0 0.0 collective-permute-done.2.refs_1_.refs_2_.refs_3_
  48.1 0.1 pad_maximum_fusion
  48.1 0.3 collective-permute-start.5
  48.4 2.2 %collective-permute-done.8.refs_0_ = bf16[256,640]{1,0:T(8,128)(2,1)S(1)} collective-permute-done((bf16[256,640]{1,0:T(8,128)(2,1)S(1)}, bf16[256,640]{1,0:T(8,128)(2,1)S(1)}, u32[]{:S(2)}, u32[]{:S(2)}) %collective-permute-start.8) | collective-permute-done | bytes 327712 | tf_op jit(solution)/shard_map/ppermute | solution.py:26
  50.6 0.0 collective-permute-done.9.refs_1_
  50.6 7.3 %near_beside.1 = (f32[512,640]{1,0:T(8,128)S(1)}, f32[512,640]{1,0:T(8,128)S(1)}, f32[512,640]{1,0:T(8,128)S(1)}) custom-call(bf16[256,640]{1,0:T(8,128)(2,1)S(1)} %collective-permute-done.8.refs_0_, bf16[256,640]{1,0:T(8,128)(2,1)S(1)} %collective-permute-done.9.refs_1_, bf16[512,640]{1,0:T(8,128)(2,1)S(1)} %copy-done.9, bf16[512,640]{1,0:T(8,128)(2,1)S(1)} %copy-done.9, ...), custom_call_target="tpu_custom_call" | custom-call | flops 5368709120 | bytes 524288 | tf_op jit(solution)/shard_map/near_beside/pallas_call | solution.py:286
  57.9 0.0 collective-permute-done.refs_0_
  57.9 4.2 %near_across.1 = (f32[256,640]{1,0:T(8,128)S(1)}, f32[256,640]{1,0:T(8,128)S(1)}, f32[256,640]{1,0:T(8,128)S(1)}) custom-call(bf16[256,640]{1,0:T(8,128)(2,1)S(1)} %collective-permute-done.refs_0_, bf16[512,640]{1,0:T(8,128)(2,1)S(1)} %copy-done.9, bf16[512,640]{1,0:T(8,128)(2,1)S(1)} %copy-done.9, bf16[512,640]{1,0:T(8,128)(2,1)S(1)} %copy-done.3, ...), custom_call_target="tpu_custom_call" | custom-call | flops 2684354560 | bytes 524288 | tf_op jit(solution)/shard_map/near_across/pallas_call | solution.py:286
  62.2 0.0 collective-permute-done.7.refs_6_.refs_8_.refs_7_.refs_9_
  62.2 1.0 collective-permute-done.5.refs_5_.refs_7_.refs_6_.refs_8_
  63.1 3.8 %far_across.1.refs_13_ = bf16[256,896]{1,0:T(8,128)(2,1)S(1)} custom-call(bf16[256,640]{1,0:T(8,128)(2,1)S(1)} %collective-permute-done.refs_0_, bf16[512,640]{1,0:T(8,128)(2,1)S(1)} %collective-permute-done.2.refs_1_.refs_2_.refs_3_, bf16[512,640]{1,0:T(8,128)(2,1)S(1)} %collective-permute-done.2.refs_1_.refs_2_.refs_3_, ...), custom_call_target="tpu_custom_call" | custom-call | flops 2684354560 | bytes 524288 | tf_op jit(solution)/shard_map/far_across/pallas_call | solution.py:286
  66.9 2.0 %collective-permute-start.10 = (bf16[256,896]{1,0:T(8,128)(2,1)S(1)}, bf16[256,896]{1,0:T(8,128)(2,1)S(1)}, u32[]{:S(2)}, u32[]{:S(2)}) collective-permute-start(bf16[256,896]{1,0:T(8,128)(2,1)S(1)} %far_across.1.refs_13_), channel_id=1, source_target_pairs={{0,4},{1,5},{2,6},{3,7},{4,0},{5,1},{6,2},{7,3},{8,12},{9,13},{10,... | collective-permute-start | bytes 1376264 | tf_op jit(solution)/shard_map/ppermute | solution.py:26
  68.9 7.3 %far_beside.1 = (bf16[256,768]{1,0:T(8,128)(2,1)S(1)}, bf16[256,768]{1,0:T(8,128)(2,1)S(1)}) custom-call(bf16[256,640]{1,0:T(8,128)(2,1)S(1)} %collective-permute-done.8.refs_0_, bf16[256,640]{1,0:T(8,128)(2,1)S(1)} %collective-permute-done.9.refs_1_, bf16[512,640]{1,0:T(8,128)(2,1)S(1)} %collective-permute-done.2.refs_1_.refs_2_.refs_3_, ...), custom_call_target="tpu_custom_call" | custom-call | flops 335544320 | bytes 32768 | tf_op jit(solution)/shard_map/far_beside/pallas_call | solution.py:286
  76.3 1.8 %collective-permute-start.11 = (bf16[256,768]{1,0:T(8,128)(2,1)S(1)}, bf16[256,768]{1,0:T(8,128)(2,1)S(1)}, u32[]{:S(2)}, u32[]{:S(2)}) collective-permute-start(bf16[256,768]{1,0:T(8,128)(2,1)S(1)} %get-tuple-element.43.refs_12_), channel_id=1, source_target_pairs={{0,6},{1,7},{2,0},{3,1},{4,2},{5,3},{6,4},{7,5},{8,14},{9,15},{10,... | collective-permute-start | bytes 1179656 | tf_op jit(solution)/shard_map/ppermute | solution.py:26
  78.1 0.2 collective-permute-start.12
  78.4 5.5 %far_own.1 = (bf16[256,768]{1,0:T(8,128)(2,1)S(1)}, bf16[9,1280,640]{2,1,0:T(8,128)(2,1)S(1)}) custom-call(bf16[256,640]{1,0:T(8,128)(2,1)S(1)} %get-tuple-element.32.refs_0_, bf16[512,640]{1,0:T(8,128)(2,1)S(1)} %collective-permute-done.2.refs_1_.refs_2_.refs_3_, bf16[512,640]{1,0:T(8,128)(2,1)S(1)} %collective-permute-done.2.refs_1_.refs_2_.refs_3_, ...), custom_call_target="tpu_custom_call" | custom-call | flops 167772160 | bytes 32768 | tf_op jit(solution)/shard_map/far_own/pallas_call | solution.py:286
  83.8 1.2 collective-permute-done.11.p1
  85.0 2.1 %collective-permute-done.12.p2 = bf16[256,768]{1,0:T(8,128)(2,1)S(1)} collective-permute-done((bf16[256,768]{1,0:T(8,128)(2,1)S(1)}, bf16[256,768]{1,0:T(8,128)(2,1)S(1)}, u32[]{:S(2)}, u32[]{:S(2)}) %collective-permute-start.12) | collective-permute-done | bytes 393248 | tf_op jit(solution)/shard_map/ppermute | solution.py:26
  87.1 0.0 collective-permute-done.10.p0
  87.1 2.5 %merge_project.1 = (f32[256,1280]{1,0:T(8,128)S(1)}, f32[32,128]{1,0:T(8,128)S(1)}) custom-call(bf16[256,896]{1,0:T(8,128)(2,1)S(1)} %collective-permute-done.10.p0, bf16[256,768]{1,0:T(8,128)(2,1)S(1)} %collective-permute-done.11.p1, bf16[256,768]{1,0:T(8,128)(2,1)S(1)} %collective-permute-done.12.p2, bf16[256,768]{1,0:T(8,128)(2,1)S(1)} %get-tuple-element.47.p3, ...), custom_call_target="tpu_custom_call" | custom-call | flops 419430400 | bytes 1638400 | tf_op jit(solution)/shard_map/merge_project/pallas_call | solution.py:330
  89.6 0.0 copy-start.8
  89.6 4.3 %collective-permute-start.13 = (f32[64,1280]{1,0:T(8,128)S(1)}, f32[64,1280]{1,0:T(8,128)S(1)}, u32[]{:S(2)}, u32[]{:S(2)}) collective-permute-start(f32[64,1280]{1,0:T(8,128)S(1)} %get-tuple-element.54), channel_id=1, source_target_pairs={{0,1},{1,2},{2,3},{3,4},{4,5},{5,6},{6,7},{7,8},{8,9},{9,10},{10,1... | collective-permute-start | bytes 983048 | tf_op jit(solution)/shard_map/ppermute | solution.py:449
  94.0 1.3 %collective-permute-start.14 = (f32[64,1280]{1,0:T(8,128)S(1)}, f32[64,1280]{1,0:T(8,128)S(1)}, u32[]{:S(2)}, u32[]{:S(2)}) collective-permute-start(f32[64,1280]{1,0:T(8,128)S(1)} %get-tuple-element.53), channel_id=1, source_target_pairs={{1,0},{2,1},{3,2},{4,3},{5,4},{6,5},{7,6},{8,7},{9,8},{10,9},{11,1... | collective-permute-start | bytes 983048 | tf_op jit(solution)/shard_map/ppermute | solution.py:450
  95.3 17.3 %all_to_all.23 = f32[32,1,128]{2,1,0:T(1,128)S(1)} all-to-all(f32[32,1,128]{2,1,0:T(1,128)S(1)} %bitcast.15), channel_id=1, replica_groups=mesh['batch'=4,'patch'=32] {'patch'}, dimensions={0} | all-to-all | bytes 32768 | tf_op jit(solution)/shard_map/all_to_all | solution.py:393
  112.5 0.0 collective-permute-done.13.above_ref
  112.5 0.0 collective-permute-done.14.below_ref
  112.5 6.2 %norm_convolve.1 = bf16[256,640]{1,0:T(8,128)(2,1)} custom-call(f32[32,128]{1,0:T(8,128)S(1)} %bitcast.14, f32[256,1280]{1,0:T(8,128)S(1)} %get-tuple-element.49.hidden_ref, f32[64,1280]{1,0:T(8,128)S(1)} %collective-permute-done.13.above_ref, f32[64,1280]{1,0:T(8,128)S(1)} %collective-permute-done.14.below_ref, f32[1280]{0:T(1024)S(1)} %copy-done.6, ...), custom_call_target="tpu_custom_call" | custom-call | flops 3774873600 | bytes 14745600 | tf_op jit(solution)/shard_map/norm_convolve/pallas_call | solution.py:378
  (23 shorter events, 0.1 us)
Async XLA Ops:
  0.6 31.5 %copy-start = (bf16[4,64,1280]{2,1,0:T(8,128)(2,1)S(1)}, bf16[4,64,1280]{2,1,0:T(8,128)(2,1)}, u32[]{:S(2)}) copy-start(bf16[4,64,1280]{2,1,0:T(8,128)(2,1)} %param.11) | copy-start | bytes 1966084
  0.6 31.5 %copy-start.7 = (f32[1280]{0:T(1024)S(1)}, f32[1280]{0:T(1024)}, u32[]{:S(2)}) copy-start(f32[1280]{0:T(1024)} %gain_ref.2) | copy-start | bytes 15364
  4.4 25.7 %collective-permute-start.1 = (bf16[512,640]{1,0:T(8,128)(2,1)}, bf16[512,640]{1,0:T(8,128)(2,1)S(1)}, u32[]{:S(2)}, u32[]{:S(2)}) collective-permute-start(bf16[512,640]{1,0:T(8,128)(2,1)} %get-tuple-element.33.refs_2_.refs_3_.refs_1_), channel_id=1, source_target_pairs={{0,1},{1,0},{2,3},{3,2},{4,5},{5,4},{6,7},{7,6},{8,9},{9,8},{10,11... | collective-permute-start | bytes 1966088 | tf_op jit(solution)/shard_map/ppermute | solution.py:26
  7.6 28.3 %collective-permute-start.4 = (bf16[512,640]{1,0:T(8,128)(2,1)}, bf16[512,640]{1,0:T(8,128)(2,1)S(1)}, u32[]{:S(2)}, u32[]{:S(2)}) collective-permute-start(bf16[512,640]{1,0:T(8,128)(2,1)} %get-tuple-element.33.refs_2_.refs_3_.refs_1_), channel_id=1, source_target_pairs={{0,8},{1,9},{2,10},{3,11},{4,12},{5,13},{6,14},{7,15},{8,16},{9,17... | collective-permute-start | bytes 1966088 | tf_op jit(solution)/shard_map/ppermute | solution.py:26
  9.2 29.1 %collective-permute-start.6 = (bf16[512,640]{1,0:T(8,128)(2,1)}, bf16[512,640]{1,0:T(8,128)(2,1)S(1)}, u32[]{:S(2)}, u32[]{:S(2)}) collective-permute-start(bf16[512,640]{1,0:T(8,128)(2,1)} %get-tuple-element.33.refs_2_.refs_3_.refs_1_), channel_id=1, source_target_pairs={{0,24},{1,25},{2,26},{3,27},{4,28},{5,29},{6,30},{7,31},{8,0},{9,1... | collective-permute-start | bytes 1966088 | tf_op jit(solution)/shard_map/ppermute | solution.py:26
  30.1 14.9 %collective-permute-start.3 = (bf16[512,640]{1,0:T(8,128)(2,1)S(1)}, bf16[512,640]{1,0:T(8,128)(2,1)S(1)}, u32[]{:S(2)}, u32[]{:S(2)}) collective-permute-start(bf16[512,640]{1,0:T(8,128)(2,1)S(1)} %collective-permute-done.1.refs_7_.refs_8_.refs_9_), channel_id=1, source_target_pairs={{0,24},{1,25},{2,26},{3,27},{4,28},{5,29},{6,30},{7,31},{8,0},{9,1... | collective-permute-start | bytes 1966088 | tf_op jit(solution)/shard_map/ppermute | solution.py:26
  31.9 16.2 %collective-permute-start.2 = (bf16[512,640]{1,0:T(8,128)(2,1)S(1)}, bf16[512,640]{1,0:T(8,128)(2,1)S(1)}, u32[]{:S(2)}, u32[]{:S(2)}) collective-permute-start(bf16[512,640]{1,0:T(8,128)(2,1)S(1)} %collective-permute-done.1.refs_7_.refs_8_.refs_9_), channel_id=1, source_target_pairs={{0,8},{1,9},{2,10},{3,11},{4,12},{5,13},{6,14},{7,15},{8,16},{9,17... | collective-permute-start | bytes 1966088 | tf_op jit(solution)/shard_map/ppermute | solution.py:26
  35.0 15.6 %collective-permute-start.8 = (bf16[256,640]{1,0:T(8,128)(2,1)S(1)}, bf16[256,640]{1,0:T(8,128)(2,1)S(1)}, u32[]{:S(2)}, u32[]{:S(2)}) collective-permute-start(bf16[256,640]{1,0:T(8,128)(2,1)S(1)} %get-tuple-element.32.refs_0_), channel_id=1, source_target_pairs={{0,2},{1,3},{2,4},{3,5},{4,6},{5,7},{6,0},{7,1},{8,10},{9,11},{10,... | collective-permute-start | bytes 983048 | tf_op jit(solution)/shard_map/ppermute | solution.py:26
  35.9 6.9 %copy-start.2 = (bf16[512,640]{1,0:T(8,128)(2,1)}, bf16[512,640]{1,0:T(8,128)(2,1)S(1)}, u32[]{:S(2)}) copy-start(bf16[512,640]{1,0:T(8,128)(2,1)S(1)} %collective-permute-done.4.refs_3_.refs_4_.refs_5_) | copy-start | bytes 1966084
  35.9 14.7 %collective-permute-start.9 = (bf16[256,640]{1,0:T(8,128)(2,1)S(1)}, bf16[256,640]{1,0:T(8,128)(2,1)S(1)}, u32[]{:S(2)}, u32[]{:S(2)}) collective-permute-start(bf16[256,640]{1,0:T(8,128)(2,1)S(1)} %get-tuple-element.32.refs_0_), channel_id=1, source_target_pairs={{0,6},{1,7},{2,0},{3,1},{4,2},{5,3},{6,4},{7,5},{8,14},{9,15},{10,... | collective-permute-start | bytes 983048 | tf_op jit(solution)/shard_map/ppermute | solution.py:26
  38.3 4.5 %copy-start.4 = (bf16[512,640]{1,0:T(8,128)(2,1)}, bf16[512,640]{1,0:T(8,128)(2,1)S(1)}, u32[]{:S(2)}) copy-start(bf16[512,640]{1,0:T(8,128)(2,1)S(1)} %collective-permute-done.6.refs_5_.refs_6_.refs_7_) | copy-start | bytes 1966084
  38.3 19.6 %collective-permute-start = (bf16[256,640]{1,0:T(8,128)(2,1)S(1)}, bf16[256,640]{1,0:T(8,128)(2,1)S(1)}, u32[]{:S(2)}, u32[]{:S(2)}) collective-permute-start(bf16[256,640]{1,0:T(8,128)(2,1)S(1)} %get-tuple-element.32.refs_0_), channel_id=1, source_target_pairs={{0,4},{1,5},{2,6},{3,7},{4,0},{5,1},{6,2},{7,3},{8,12},{9,13},{10,... | collective-permute-start | bytes 983048 | tf_op jit(solution)/shard_map/ppermute | solution.py:26
  42.8 2.3 %slice-start.1 = ((bf16[512,640]{1,0:T(8,128)(2,1)}), bf16[256,640]{1,0:T(8,128)(2,1)S(1)}, s32[]{:S(2)}) async-start(bf16[512,640]{1,0:T(8,128)(2,1)} %copy-done.4), calls=%async_computation.3 | async-start | bytes 655360 | tf_op jit(solution)/shard_map/slice | solution.py:426
  42.8 5.3 %slice-start = ((bf16[512,640]{1,0:T(8,128)(2,1)}), bf16[256,640]{1,0:T(8,128)(2,1)S(1)}, s32[]{:S(2)}) async-start(bf16[512,640]{1,0:T(8,128)(2,1)} %copy-done.2), calls=%async_computation.2 | async-start | bytes 655360 | tf_op jit(solution)/shard_map/slice | solution.py:425
  45.1 5.5 %copy-start.3 = (bf16[512,640]{1,0:T(8,128)(2,1)S(1)}, bf16[512,640]{1,0:T(8,128)(2,1)}, u32[]{:S(2)}) copy-start(bf16[512,640]{1,0:T(8,128)(2,1)} %copy-done.2) | copy-start | bytes 1966084
  45.1 5.5 %copy-start.5 = (bf16[512,640]{1,0:T(8,128)(2,1)S(1)}, bf16[512,640]{1,0:T(8,128)(2,1)}, u32[]{:S(2)}) copy-start(bf16[512,640]{1,0:T(8,128)(2,1)} %copy-done.4) | copy-start | bytes 1966084
  45.2 5.5 %copy-start.9 = (bf16[512,640]{1,0:T(8,128)(2,1)S(1)}, bf16[512,640]{1,0:T(8,128)(2,1)}, u32[]{:S(2)}) copy-start(bf16[512,640]{1,0:T(8,128)(2,1)} %get-tuple-element.33.refs_2_.refs_3_.refs_1_) | copy-start | bytes 1966084
  45.2 17.0 %collective-permute-start.7 = (bf16[512,640]{1,0:T(8,128)(2,1)S(1)}, bf16[512,640]{1,0:T(8,128)(2,1)S(1)}, u32[]{:S(2)}, u32[]{:S(2)}) collective-permute-start(bf16[512,640]{1,0:T(8,128)(2,1)S(1)} %pad_maximum_fusion.1), channel_id=1, source_target_pairs={{0,24},{1,25},{2,26},{3,27},{4,28},{5,29},{6,30},{7,31},{8,0},{9,1... | collective-permute-start | bytes 1966088 | tf_op jit(solution)/shard_map/ppermute | solution.py:26
  48.1 15.0 %collective-permute-start.5 = (bf16[512,640]{1,0:T(8,128)(2,1)S(1)}, bf16[512,640]{1,0:T(8,128)(2,1)S(1)}, u32[]{:S(2)}, u32[]{:S(2)}) collective-permute-start(bf16[512,640]{1,0:T(8,128)(2,1)S(1)} %pad_maximum_fusion), channel_id=1, source_target_pairs={{0,8},{1,9},{2,10},{3,11},{4,12},{5,13},{6,14},{7,15},{8,16},{9,17... | collective-permute-start | bytes 1966088 | tf_op jit(solution)/shard_map/ppermute | solution.py:26
  66.9 20.2 %collective-permute-start.10 = (bf16[256,896]{1,0:T(8,128)(2,1)S(1)}, bf16[256,896]{1,0:T(8,128)(2,1)S(1)}, u32[]{:S(2)}, u32[]{:S(2)}) collective-permute-start(bf16[256,896]{1,0:T(8,128)(2,1)S(1)} %far_across.1.refs_13_), channel_id=1, source_target_pairs={{0,4},{1,5},{2,6},{3,7},{4,0},{5,1},{6,2},{7,3},{8,12},{9,13},{10,... | collective-permute-start | bytes 1376264 | tf_op jit(solution)/shard_map/ppermute | solution.py:26
  76.3 8.7 %collective-permute-start.11 = (bf16[256,768]{1,0:T(8,128)(2,1)S(1)}, bf16[256,768]{1,0:T(8,128)(2,1)S(1)}, u32[]{:S(2)}, u32[]{:S(2)}) collective-permute-start(bf16[256,768]{1,0:T(8,128)(2,1)S(1)} %get-tuple-element.43.refs_12_), channel_id=1, source_target_pairs={{0,6},{1,7},{2,0},{3,1},{4,2},{5,3},{6,4},{7,5},{8,14},{9,15},{10,... | collective-permute-start | bytes 1179656 | tf_op jit(solution)/shard_map/ppermute | solution.py:26
  78.1 9.0 %collective-permute-start.12 = (bf16[256,768]{1,0:T(8,128)(2,1)S(1)}, bf16[256,768]{1,0:T(8,128)(2,1)S(1)}, u32[]{:S(2)}, u32[]{:S(2)}) collective-permute-start(bf16[256,768]{1,0:T(8,128)(2,1)S(1)} %get-tuple-element.44), channel_id=1, source_target_pairs={{0,2},{1,3},{2,4},{3,5},{4,6},{5,7},{6,0},{7,1},{8,10},{9,11},{10,... | collective-permute-start | bytes 1179656 | tf_op jit(solution)/shard_map/ppermute | solution.py:26
  78.4 8.7 %copy-start.1 = (bf16[640,1280]{1,0:T(8,128)(2,1)S(1)}, bf16[640,1280]{1,0:T(8,128)(2,1)}, u32[]{:S(2)}) copy-start(bf16[640,1280]{1,0:T(8,128)(2,1)} %w_ref.1) | copy-start | bytes 4915204
  89.5 23.0 %copy-start.6 = (f32[1280]{0:T(1024)S(1)}, f32[1280]{0:T(1024)}, u32[]{:S(2)}) copy-start(f32[1280]{0:T(1024)} %gain_ref.3) | copy-start | bytes 15364
  89.6 23.0 %copy-start.8 = (f32[640]{0:T(1024)S(1)}, f32[640]{0:T(1024)}, u32[]{:S(2)}) copy-start(f32[640]{0:T(1024)} %shift_ref.1) | copy-start | bytes 7684
  89.6 22.9 %collective-permute-start.13 = (f32[64,1280]{1,0:T(8,128)S(1)}, f32[64,1280]{1,0:T(8,128)S(1)}, u32[]{:S(2)}, u32[]{:S(2)}) collective-permute-start(f32[64,1280]{1,0:T(8,128)S(1)} %get-tuple-element.54), channel_id=1, source_target_pairs={{0,1},{1,2},{2,3},{3,4},{4,5},{5,6},{6,7},{7,8},{8,9},{9,10},{10,1... | collective-permute-start | bytes 983048 | tf_op jit(solution)/shard_map/ppermute | solution.py:449
  94.0 18.6 %collective-permute-start.14 = (f32[64,1280]{1,0:T(8,128)S(1)}, f32[64,1280]{1,0:T(8,128)S(1)}, u32[]{:S(2)}, u32[]{:S(2)}) collective-permute-start(f32[64,1280]{1,0:T(8,128)S(1)} %get-tuple-element.53), channel_id=1, source_target_pairs={{1,0},{2,1},{3,2},{4,3},{5,4},{6,5},{7,6},{8,7},{9,8},{10,9},{11,1... | collective-permute-start | bytes 983048 | tf_op jit(solution)/shard_map/ppermute | solution.py:450

commit v2 on v1

--- a/solution.py
+++ b/solution.py
@@ -10,6 +10,7 @@
 HEAD = 64
 GROUPS = 32
 LANES = 128
+EXTRA = 32
 NY, NZ, NX = 4, 4, 2
 EPS = 1e-05
 BF = jnp.bfloat16
@@ -186,6 +187,7 @@
     copies = []
     (kept,) = take(1) if carry else (None,)
     (scores,) = take(1)
+    (levels,) = take(1) if final else (None,)
     if carry:
         (sems,) = take(1)
         copies = [
@@ -197,8 +199,9 @@
     lane = lax.broadcasted_iota(jnp.int32, (rows, LANES), 1)
     ones = jnp.ones((rows, LANES), BF)
     if final:
+        levels[...] = jnp.zeros(levels.shape, F32)
         for o_ref in outs:
-            o_ref[:, width:] = jnp.zeros((rows, o_ref.shape[1] - width), BF)
+            o_ref[rows:, :] = jnp.zeros((o_ref.shape[0] - rows, width), BF)
 
     pairs = width // LANES
     lanes_of = lambda j: pl.ds(pl.multiple_of(j * LANES, LANES), LANES)
@@ -237,18 +240,15 @@
                 for out_ref, value in zip(outs, (summed, top, total)):
                     out_ref[at, cols] = value
                 continue
-            outs[band][:, cols] = (summed / total).astype(BF)
+            outs[band][0:rows, cols] = (summed / total).astype(BF)
             level = top + jnp.log(total)
-            swapped = pltpu.roll(level, HEAD, 1)
-            row_level = (jnp.where(first, level, swapped), jnp.where(first, swapped, level))
-            extra = outs[band][:, width : width + LANES]
+            turned = level.T
             for h in range(2):
-                rest = row_level[h]
+                rest = turned[h * HEAD : h * HEAD + 1, :]
                 for cut in range(3):
-                    part = rest.astype(BF)
-                    rest = rest - part.astype(F32)
-                    extra = jnp.where(lane == 2 * j + h + 10 * cut, part, extra)
-            outs[band][:, width : width + LANES] = extra
+                    part = rest.astype(BF).astype(F32)
+                    rest = rest - part
+                    levels[band, pl.ds(10 * cut + 2 * j + h, 1), :] = part
 
     start_keys = keys_of(slice(0, LANES))
     for band, q_ref in enumerate(queries):
@@ -261,11 +261,14 @@
 
     lax.fori_loop(0, pairs - 1, loop_step, 0, unroll=unroll)
     step(pairs - 1, False)
+    if final:
+        for band, o_ref in enumerate(outs):
+            o_ref[rows : rows + EXTRA, 0:rows] = levels[band].astype(BF)
     for copy in copies:
         copy.wait()
 
 
-def attend(name, queries, blocks, state=None, final=False, after=(), carry=None, weight=16, extra=1, unroll=False):
+def attend(name, queries, blocks, state=None, final=False, after=(), carry=None, weight=16, extra=0, unroll=False):
     rows, width = queries[0].shape
     count = len(queries)
     sources = []
@@ -273,10 +276,12 @@
         sources += [keys, values]
     plan = (count, [(key_row, value_row) for _, key_row, _, value_row in blocks])
     if final:
-        out_shape = [jax.ShapeDtypeStruct((rows, width + extra * LANES), BF)] * count
+        out_shape = [jax.ShapeDtypeStruct((rows + EXTRA + extra, width), BF)] * count
     else:
         out_shape = [jax.ShapeDtypeStruct((count * rows, width), F32)] * 3
     scratch = [pltpu.VMEM((2 * count, rows, len(blocks) * rows), F32)]
+    if final:
+        scratch.append(pltpu.VMEM((count, EXTRA, rows), F32))
     carried = []
     if carry is not None:
         out_shape.append(pltpu.VMEM(carry.shape, carry.dtype))
@@ -303,21 +308,27 @@
 
 def merge_kernel(p0, p1, p2, p3, x_ref, w_ref, hidden_ref, stats_ref):
     width = w_ref.shape[0]
-    lane = lax.broadcasted_iota(jnp.int32, (LANES, width), 0)
-    chan = lax.broadcasted_iota(jnp.int32, (LANES, width), 1)
-    spread = jnp.zeros((LANES, width), F32)
-    for piece in range(3):
-        head = lane - 10 * piece
+    rows = x_ref.shape[0]
+    row = lax.broadcasted_iota(jnp.int32, (EXTRA, width), 0)
+    chan = lax.broadcasted_iota(jnp.int32, (EXTRA, width), 1)
+    spread = jnp.zeros((EXTRA, width), F32)
+    for cut in range(3):
+        head = row - 10 * cut
         inside = (head >= 0) & (head < 10) & (chan >= head * HEAD) & (chan < head * HEAD + HEAD)
         spread = jnp.where(inside, 1.0, spread)
     spread = spread.astype(BF)
     parts = (p0, p1, p2, p3)
-    levels = [jnp.dot(p[:, width : width + LANES], spread, preferred_element_type=F32) for p in parts]
+    levels = [
+        lax.dot_general(
+            p[rows : rows + EXTRA, 0:rows], spread, (((0,), (0,)), ((), ())), preferred_element_type=F32
+        )
+        for p in parts
+    ]
     top = functools.reduce(jnp.maximum, levels)
     shares = [jnp.exp(level - top) for level in levels]
     total = functools.reduce(jnp.add, shares)
     summed = functools.reduce(
-        jnp.add, [s * p[:, :width].astype(F32) for s, p in zip(shares, parts)]
+        jnp.add, [s * p[0:rows, :].astype(F32) for s, p in zip(shares, parts)]
     )
     attended = (summed / total).astype(BF)
     hidden = x_ref[...].astype(F32) + jnp.dot(attended, w_ref[...], preferred_element_type=F32)
@@ -431,8 +442,8 @@
     far += [(last_keys, 0, last_values, 0), (last_keys, 1, last_values, 1)]
     own_state = attend("near_own", [queries], [whole(fresh)] + near)
     beside_state = attend("near_beside", beside, [whole(old)] + near, after=own_state[1:2])
-    across_state = attend("near_across", across, [whole(old)] + near, after=beside_state[1:2])
-    (to_across,) = attend("far_across", across, far, across_state, final=True, extra=2, unroll=True)
+    across_state = attend("near_across", across, [whole(old)] + near, after=beside_state[1:2], unroll=True)
+    (to_across,) = attend("far_across", across, far, across_state, final=True, extra=16, unroll=True)
     from_across = shifted(to_across, 0, 2, 0)
     to_beside = attend("far_beside", beside, far, beside_state, final=True, after=(to_across,), weight=1, unroll=True)
     own_part, weight = attend(

time: 119 us -> 118 us (level)
  transfers between devices with their start and end apart: 15 -> 15, of which waited for: 5 -> 4; matrix products, arithmetic and copies ran while one was open for 0% -> 0% of each run, Pallas kernels for 26% -> 26%
where the time goes in v2:
time: 118 us
  Pallas kernels  47.1 us (40%)
  blocking collectives  35.7 us (30%)
  starting transfers between devices  24.8 us (21%)
  waiting for transfers between devices  9.21 us (8%)
    all_to_all x2, blocking collectives, everyones(): return lax.all_to_all(stats, 'patch', 0, 0, tiled=True)  35.7 us
    pallas_call x6, Pallas kernels, attend(): pl.pallas_call(functools.partial(attend_kernel, plan, bool(state), final,...  31.7 us
    ppermute x13, starting transfers between devices, shifted(): return lax.ppermute(x, 'patch', pairs)  19.1 us
    ppermute x13, waiting for transfers between devices, shifted(): return lax.ppermute(x, 'patch', pairs)  9.2 us
    pallas_call x1, Pallas kernels, convolve(): pl.pallas_call(conv_kernel, in_specs=[VMEM] * 7, out_specs=VMEM, out_shap...  6.21 us
    ppermute x1, starting transfers between devices, shards(): above = lax.ppermute(hidden[tok_count - col_count:], 'patch', down)  4.34 us
    pallas_call x1, Pallas kernels, norm_stats(): pl.pallas_call(stats_kernel, in_specs=[HBM] * 6, out_specs=[VMEM] * 5, ou...  3.77 us
    pallas_call x1, Pallas kernels, project(): pl.pallas_call(project_kernel, in_specs=[VMEM] * 6, out_specs=[VMEM] * 4,...  2.92 us
  transfers between devices with their start and end apart: 15, of which 4 were waited for; matrix products, arithmetic and copies ran while one was open for 0% of the time, Pallas kernels for 26%

profile of v2, /device:TPU:0, one launch (start us, length us, event | category | flops | bytes accessed | tf_op | source)
XLA Modules:
  0.0 118.0 jit_solution(8831236364207288493)
XLA Ops:
  0.7 3.8 %norm_stats.1 = (f32[32,128]{1,0:T(8,128)}, bf16[512,640]{1,0:T(8,128)(2,1)}, bf16[1280,640]{1,0:T(8,128)(2,1)S(1)}, bf16[1280,640]{1,0:T(8,128)(2,1)S(1)}, bf16[1280,640]{1,0:T(8,128)(2,1)S(1)}) custom-call(bf16[256,1280]{1,0:T(8,128)(2,1)} %bitcast.10, bf16[256,640]{1,0:T(8,128)(2,1)} %k_ref.1, bf16[256,640]{1,0:T(8,128)(2,1)} %v_ref.1, ...), custom_call_target="tpu_custom_call" | custom-call | flops 1310720 | bytes 655360 | tf_op jit(solution)/shard_map/norm_stats/pallas_call | solution.py:118
  4.4 3.2 %collective-permute-start.1 = (bf16[512,640]{1,0:T(8,128)(2,1)}, bf16[512,640]{1,0:T(8,128)(2,1)S(1)}, u32[]{:S(2)}, u32[]{:S(2)}) collective-permute-start(bf16[512,640]{1,0:T(8,128)(2,1)} %get-tuple-element.33.refs_2_.refs_3_.refs_1_), channel_id=1, source_target_pairs={{0,1},{1,0},{2,3},{3,2},{4,5},{5,4},{6,7},{7,6},{8,9},{9,8},{10,11... | collective-permute-start | bytes 1966088 | tf_op jit(solution)/shard_map/ppermute | solution.py:27
  7.6 1.6 %collective-permute-start.4 = (bf16[512,640]{1,0:T(8,128)(2,1)}, bf16[512,640]{1,0:T(8,128)(2,1)S(1)}, u32[]{:S(2)}, u32[]{:S(2)}) collective-permute-start(bf16[512,640]{1,0:T(8,128)(2,1)} %get-tuple-element.33.refs_2_.refs_3_.refs_1_), channel_id=1, source_target_pairs={{0,8},{1,9},{2,10},{3,11},{4,12},{5,13},{6,14},{7,15},{8,16},{9,17... | collective-permute-start | bytes 1966088 | tf_op jit(solution)/shard_map/ppermute | solution.py:27
  9.2 1.7 %collective-permute-start.6 = (bf16[512,640]{1,0:T(8,128)(2,1)}, bf16[512,640]{1,0:T(8,128)(2,1)S(1)}, u32[]{:S(2)}, u32[]{:S(2)}) collective-permute-start(bf16[512,640]{1,0:T(8,128)(2,1)} %get-tuple-element.33.refs_2_.refs_3_.refs_1_), channel_id=1, source_target_pairs={{0,24},{1,25},{2,26},{3,27},{4,28},{5,29},{6,30},{7,31},{8,0},{9,1... | collective-permute-start | bytes 1966088 | tf_op jit(solution)/shard_map/ppermute | solution.py:27
  10.9 19.2 %all_to_all.22 = f32[32,1,128]{2,1,0:T(1,128)S(1)} all-to-all(f32[32,1,128]{2,1,0:T(1,128)} %bitcast.17), channel_id=1, replica_groups=mesh['batch'=4,'patch'=32] {'patch'}, dimensions={0} | all-to-all | bytes 32768 | tf_op jit(solution)/shard_map/all_to_all | solution.py:404
  30.1 0.0 collective-permute-done.1.refs_7_.refs_8_.refs_9_
  30.1 1.8 %collective-permute-start.3 = (bf16[512,640]{1,0:T(8,128)(2,1)S(1)}, bf16[512,640]{1,0:T(8,128)(2,1)S(1)}, u32[]{:S(2)}, u32[]{:S(2)}) collective-permute-start(bf16[512,640]{1,0:T(8,128)(2,1)S(1)} %collective-permute-done.1.refs_7_.refs_8_.refs_9_), channel_id=1, source_target_pairs={{0,24},{1,25},{2,26},{3,27},{4,28},{5,29},{6,30},{7,31},{8,0},{9,1... | collective-permute-start | bytes 1966088 | tf_op jit(solution)/shard_map/ppermute | solution.py:27
  31.9 0.2 collective-permute-start.2
  32.1 0.0 copy-done
  32.1 2.9 %project.1 = (bf16[256,640]{1,0:T(8,128)(2,1)S(1)}, bf16[256,640]{1,0:T(8,128)(2,1)}, bf16[256,640]{1,0:T(8,128)(2,1)}, bf16[512,640]{1,0:T(8,128)(2,1)S(1)}) custom-call(f32[32,128]{1,0:T(8,128)S(1)} %bitcast.13, bf16[256,1280]{1,0:T(8,128)(2,1)S(1)} %bitcast.11, f32[1280]{0:T(1024)S(1)} %copy-done.7, bf16[1280,640]{1,0:T(8,128)(2,1)S(1)} %get-tuple-element.29.wq, ...), custom_call_target="tpu_custom_call" | custom-call | flops 1258291200 | bytes 4915200 | tf_op jit(solution)/shard_map/project/pallas_call | solution.py:149
  35.0 0.8 collective-permute-start.8
  35.9 0.0 collective-permute-done.4.refs_3_.refs_4_.refs_5_
  35.9 2.4 %collective-permute-start.9 = (bf16[256,640]{1,0:T(8,128)(2,1)S(1)}, bf16[256,640]{1,0:T(8,128)(2,1)S(1)}, u32[]{:S(2)}, u32[]{:S(2)}) collective-permute-start(bf16[256,640]{1,0:T(8,128)(2,1)S(1)} %get-tuple-element.32.refs_0_), channel_id=1, source_target_pairs={{0,6},{1,7},{2,0},{3,1},{4,2},{5,3},{6,4},{7,5},{8,14},{9,15},{10,... | collective-permute-start | bytes 983048 | tf_op jit(solution)/shard_map/ppermute | solution.py:27
  38.3 0.0 collective-permute-done.6.refs_5_.refs_6_.refs_7_
  38.3 0.2 collective-permute-start
  38.5 4.2 %near_own.1 = (f32[256,640]{1,0:T(8,128)S(1)}, f32[256,640]{1,0:T(8,128)S(1)}, f32[256,640]{1,0:T(8,128)S(1)}) custom-call(bf16[256,640]{1,0:T(8,128)(2,1)S(1)} %get-tuple-element.32.refs_0_, bf16[512,640]{1,0:T(8,128)(2,1)S(1)} %get-tuple-element.35.refs_1_.refs_2_, bf16[512,640]{1,0:T(8,128)(2,1)S(1)} %get-tuple-element.35.refs_1_.refs_2_, ...), custom_call_target="tpu_custom_call" | custom-call | flops 2684354560 | bytes 524288 | tf_op jit(solution)/shard_map/near_own/pallas_call | solution.py:291
  42.8 0.0 slice-start.1
  42.8 0.0 slice-start
  42.8 2.2 %collective-permute-done.3.refs_3_.refs_4_.refs_5_ = bf16[512,640]{1,0:T(8,128)(2,1)S(1)} collective-permute-done((bf16[512,640]{1,0:T(8,128)(2,1)S(1)}, bf16[512,640]{1,0:T(8,128)(2,1)S(1)}, u32[]{:S(2)}, u32[]{:S(2)}) %collective-permute-start.3) | collective-permute-done | bytes 655392 | tf_op jit(solution)/shard_map/ppermute | solution.py:27
  45.1 0.1 pad_maximum_fusion.1
  45.2 2.9 %collective-permute-start.7 = (bf16[512,640]{1,0:T(8,128)(2,1)S(1)}, bf16[512,640]{1,0:T(8,128)(2,1)S(1)}, u32[]{:S(2)}, u32[]{:S(2)}) collective-permute-start(bf16[512,640]{1,0:T(8,128)(2,1)S(1)} %pad_maximum_fusion.1), channel_id=1, source_target_pairs={{0,24},{1,25},{2,26},{3,27},{4,28},{5,29},{6,30},{7,31},{8,0},{9,1... | collective-permute-start | bytes 1966088 | tf_op jit(solution)/shard_map/ppermute | solution.py:27
  48.0 0.0 collective-permute-done.2.refs_1_.refs_2_.refs_3_
  48.1 0.1 pad_maximum_fusion
  48.1 0.3 collective-permute-start.5
  48.4 2.2 %collective-permute-done.8.refs_0_ = bf16[256,640]{1,0:T(8,128)(2,1)S(1)} collective-permute-done((bf16[256,640]{1,0:T(8,128)(2,1)S(1)}, bf16[256,640]{1,0:T(8,128)(2,1)S(1)}, u32[]{:S(2)}, u32[]{:S(2)}) %collective-permute-start.8) | collective-permute-done | bytes 327712 | tf_op jit(solution)/shard_map/ppermute | solution.py:27
  50.6 0.0 collective-permute-done.9.refs_1_
  50.6 7.3 %near_beside.1 = (f32[512,640]{1,0:T(8,128)S(1)}, f32[512,640]{1,0:T(8,128)S(1)}, f32[512,640]{1,0:T(8,128)S(1)}) custom-call(bf16[256,640]{1,0:T(8,128)(2,1)S(1)} %collective-permute-done.8.refs_0_, bf16[256,640]{1,0:T(8,128)(2,1)S(1)} %collective-permute-done.9.refs_1_, bf16[512,640]{1,0:T(8,128)(2,1)S(1)} %copy-done.9, bf16[512,640]{1,0:T(8,128)(2,1)S(1)} %copy-done.9, ...), custom_call_target="tpu_custom_call" | custom-call | flops 5368709120 | bytes 524288 | tf_op jit(solution)/shard_map/near_beside/pallas_call | solution.py:291
  57.9 0.0 collective-permute-done.refs_0_
  57.9 3.4 %near_across.1 = (f32[256,640]{1,0:T(8,128)S(1)}, f32[256,640]{1,0:T(8,128)S(1)}, f32[256,640]{1,0:T(8,128)S(1)}) custom-call(bf16[256,640]{1,0:T(8,128)(2,1)S(1)} %collective-permute-done.refs_0_, bf16[512,640]{1,0:T(8,128)(2,1)S(1)} %copy-done.9, bf16[512,640]{1,0:T(8,128)(2,1)S(1)} %copy-done.9, bf16[512,640]{1,0:T(8,128)(2,1)S(1)} %copy-done.3, ...), custom_call_target="tpu_custom_call" | custom-call | flops 2684354560 | bytes 524288 | tf_op jit(solution)/shard_map/near_across/pallas_call | solution.py:291
  61.4 0.0 collective-permute-done.7.refs_6_.refs_8_.refs_7_.refs_9_
  61.4 1.7 %collective-permute-done.5.refs_5_.refs_7_.refs_6_.refs_8_ = bf16[512,640]{1,0:T(8,128)(2,1)S(1)} collective-permute-done((bf16[512,640]{1,0:T(8,128)(2,1)S(1)}, bf16[512,640]{1,0:T(8,128)(2,1)S(1)}, u32[]{:S(2)}, u32[]{:S(2)}) %collective-permute-start.5) | collective-permute-done | bytes 655392 | tf_op jit(solution)/shard_map/ppermute | solution.py:27
  63.1 3.8 %far_across.1.refs_13_ = bf16[304,640]{1,0:T(8,128)(2,1)S(1)} custom-call(bf16[256,640]{1,0:T(8,128)(2,1)S(1)} %collective-permute-done.refs_0_, bf16[512,640]{1,0:T(8,128)(2,1)S(1)} %collective-permute-done.2.refs_1_.refs_2_.refs_3_, bf16[512,640]{1,0:T(8,128)(2,1)S(1)} %collective-permute-done.2.refs_1_.refs_2_.refs_3_, ...), custom_call_target="tpu_custom_call" | custom-call | flops 2684354560 | bytes 524288 | tf_op jit(solution)/shard_map/far_across/pallas_call | solution.py:291
  67.0 2.0 %collective-permute-start.10 = (bf16[304,640]{1,0:T(8,128)(2,1)S(1)}, bf16[304,640]{1,0:T(8,128)(2,1)S(1)}, u32[]{:S(2)}, u32[]{:S(2)}) collective-permute-start(bf16[304,640]{1,0:T(8,128)(2,1)S(1)} %far_across.1.refs_13_), channel_id=1, source_target_pairs={{0,4},{1,5},{2,6},{3,7},{4,0},{5,1},{6,2},{7,3},{8,12},{9,13},{10,... | collective-permute-start | bytes 1167368 | tf_op jit(solution)/shard_map/ppermute | solution.py:27
  69.0 7.5 %far_beside.1 = (bf16[288,640]{1,0:T(8,128)(2,1)S(1)}, bf16[288,640]{1,0:T(8,128)(2,1)S(1)}) custom-call(bf16[256,640]{1,0:T(8,128)(2,1)S(1)} %collective-permute-done.8.refs_0_, bf16[256,640]{1,0:T(8,128)(2,1)S(1)} %collective-permute-done.9.refs_1_, bf16[512,640]{1,0:T(8,128)(2,1)S(1)} %collective-permute-done.2.refs_1_.refs_2_.refs_3_, ...), custom_call_target="tpu_custom_call" | custom-call | flops 335544320 | bytes 32768 | tf_op jit(solution)/shard_map/far_beside/pallas_call | solution.py:291
  76.4 1.8 %collective-permute-start.11 = (bf16[288,640]{1,0:T(8,128)(2,1)S(1)}, bf16[288,640]{1,0:T(8,128)(2,1)S(1)}, u32[]{:S(2)}, u32[]{:S(2)}) collective-permute-start(bf16[288,640]{1,0:T(8,128)(2,1)S(1)} %get-tuple-element.43.refs_12_), channel_id=1, source_target_pairs={{0,6},{1,7},{2,0},{3,1},{4,2},{5,3},{6,4},{7,5},{8,14},{9,15},{10,... | collective-permute-start | bytes 1105928 | tf_op jit(solution)/shard_map/ppermute | solution.py:27
  78.3 0.2 collective-permute-start.12
  78.5 5.5 %far_own.1 = (bf16[288,640]{1,0:T(8,128)(2,1)S(1)}, bf16[9,1280,640]{2,1,0:T(8,128)(2,1)S(1)}) custom-call(bf16[256,640]{1,0:T(8,128)(2,1)S(1)} %get-tuple-element.32.refs_0_, bf16[512,640]{1,0:T(8,128)(2,1)S(1)} %collective-permute-done.2.refs_1_.refs_2_.refs_3_, bf16[512,640]{1,0:T(8,128)(2,1)S(1)} %collective-permute-done.2.refs_1_.refs_2_.refs_3_, ...), custom_call_target="tpu_custom_call" | custom-call | flops 167772160 | bytes 32768 | tf_op jit(solution)/shard_map/far_own/pallas_call | solution.py:291
  84.0 0.0 collective-permute-done.11.p1
  84.0 3.0 %collective-permute-done.12.p2 = bf16[288,640]{1,0:T(8,128)(2,1)S(1)} collective-permute-done((bf16[288,640]{1,0:T(8,128)(2,1)S(1)}, bf16[288,640]{1,0:T(8,128)(2,1)S(1)}, u32[]{:S(2)}, u32[]{:S(2)}) %collective-permute-start.12) | collective-permute-done | bytes 368672 | tf_op jit(solution)/shard_map/ppermute | solution.py:27
  87.0 0.0 collective-permute-done.10.p0
  87.0 2.5 %merge_project.1 = (f32[256,1280]{1,0:T(8,128)S(1)}, f32[32,128]{1,0:T(8,128)S(1)}) custom-call(bf16[304,640]{1,0:T(8,128)(2,1)S(1)} %collective-permute-done.10.p0, bf16[288,640]{1,0:T(8,128)(2,1)S(1)} %collective-permute-done.11.p1, bf16[288,640]{1,0:T(8,128)(2,1)S(1)} %collective-permute-done.12.p2, bf16[288,640]{1,0:T(8,128)(2,1)S(1)} %get-tuple-element.47.p3, ...), custom_call_target="tpu_custom_call" | custom-call | flops 419430400 | bytes 1638400 | tf_op jit(solution)/shard_map/merge_project/pallas_call | solution.py:341
  89.5 0.0 copy-start.8
  89.6 4.3 %collective-permute-start.13 = (f32[64,1280]{1,0:T(8,128)S(1)}, f32[64,1280]{1,0:T(8,128)S(1)}, u32[]{:S(2)}, u32[]{:S(2)}) collective-permute-start(f32[64,1280]{1,0:T(8,128)S(1)} %get-tuple-element.54), channel_id=1, source_target_pairs={{0,1},{1,2},{2,3},{3,4},{4,5},{5,6},{6,7},{7,8},{8,9},{9,10},{10,1... | collective-permute-start | bytes 983048 | tf_op jit(solution)/shard_map/ppermute | solution.py:460
  94.0 1.3 %collective-permute-start.14 = (f32[64,1280]{1,0:T(8,128)S(1)}, f32[64,1280]{1,0:T(8,128)S(1)}, u32[]{:S(2)}, u32[]{:S(2)}) collective-permute-start(f32[64,1280]{1,0:T(8,128)S(1)} %get-tuple-element.53), channel_id=1, source_target_pairs={{1,0},{2,1},{3,2},{4,3},{5,4},{6,5},{7,6},{8,7},{9,8},{10,9},{11,1... | collective-permute-start | bytes 983048 | tf_op jit(solution)/shard_map/ppermute | solution.py:461
  95.3 16.5 %all_to_all.23 = f32[32,1,128]{2,1,0:T(1,128)S(1)} all-to-all(f32[32,1,128]{2,1,0:T(1,128)S(1)} %bitcast.15), channel_id=1, replica_groups=mesh['batch'=4,'patch'=32] {'patch'}, dimensions={0} | all-to-all | bytes 32768 | tf_op jit(solution)/shard_map/all_to_all | solution.py:404
  111.7 0.0 collective-permute-done.13.above_ref
  111.7 0.0 collective-permute-done.14.below_ref
  111.8 6.2 %norm_convolve.1 = bf16[256,640]{1,0:T(8,128)(2,1)} custom-call(f32[32,128]{1,0:T(8,128)S(1)} %bitcast.14, f32[256,1280]{1,0:T(8,128)S(1)} %get-tuple-element.49.hidden_ref, f32[64,1280]{1,0:T(8,128)S(1)} %collective-permute-done.13.above_ref, f32[64,1280]{1,0:T(8,128)S(1)} %collective-permute-done.14.below_ref, f32[1280]{0:T(1024)S(1)} %copy-done.6, ...), custom_call_target="tpu_custom_call" | custom-call | flops 3774873600 | bytes 14745600 | tf_op jit(solution)/shard_map/norm_convolve/pallas_call | solution.py:389
  (23 shorter events, 0.1 us)
Async XLA Ops:
  0.6 31.5 %copy-start = (bf16[4,64,1280]{2,1,0:T(8,128)(2,1)S(1)}, bf16[4,64,1280]{2,1,0:T(8,128)(2,1)}, u32[]{:S(2)}) copy-start(bf16[4,64,1280]{2,1,0:T(8,128)(2,1)} %param.11) | copy-start | bytes 1966084
  0.6 31.5 %copy-start.7 = (f32[1280]{0:T(1024)S(1)}, f32[1280]{0:T(1024)}, u32[]{:S(2)}) copy-start(f32[1280]{0:T(1024)} %gain_ref.2) | copy-start | bytes 15364
  4.4 25.7 %collective-permute-start.1 = (bf16[512,640]{1,0:T(8,128)(2,1)}, bf16[512,640]{1,0:T(8,128)(2,1)S(1)}, u32[]{:S(2)}, u32[]{:S(2)}) collective-permute-start(bf16[512,640]{1,0:T(8,128)(2,1)} %get-tuple-element.33.refs_2_.refs_3_.refs_1_), channel_id=1, source_target_pairs={{0,1},{1,0},{2,3},{3,2},{4,5},{5,4},{6,7},{7,6},{8,9},{9,8},{10,11... | collective-permute-start | bytes 1966088 | tf_op jit(solution)/shard_map/ppermute | solution.py:27
  7.6 28.3 %collective-permute-start.4 = (bf16[512,640]{1,0:T(8,128)(2,1)}, bf16[512,640]{1,0:T(8,128)(2,1)S(1)}, u32[]{:S(2)}, u32[]{:S(2)}) collective-permute-start(bf16[512,640]{1,0:T(8,128)(2,1)} %get-tuple-element.33.refs_2_.refs_3_.refs_1_), channel_id=1, source_target_pairs={{0,8},{1,9},{2,10},{3,11},{4,12},{5,13},{6,14},{7,15},{8,16},{9,17... | collective-permute-start | bytes 1966088 | tf_op jit(solution)/shard_map/ppermute | solution.py:27
  9.2 29.1 %collective-permute-start.6 = (bf16[512,640]{1,0:T(8,128)(2,1)}, bf16[512,640]{1,0:T(8,128)(2,1)S(1)}, u32[]{:S(2)}, u32[]{:S(2)}) collective-permute-start(bf16[512,640]{1,0:T(8,128)(2,1)} %get-tuple-element.33.refs_2_.refs_3_.refs_1_), channel_id=1, source_target_pairs={{0,24},{1,25},{2,26},{3,27},{4,28},{5,29},{6,30},{7,31},{8,0},{9,1... | collective-permute-start | bytes 1966088 | tf_op jit(solution)/shard_map/ppermute | solution.py:27
  30.1 14.9 %collective-permute-start.3 = (bf16[512,640]{1,0:T(8,128)(2,1)S(1)}, bf16[512,640]{1,0:T(8,128)(2,1)S(1)}, u32[]{:S(2)}, u32[]{:S(2)}) collective-permute-start(bf16[512,640]{1,0:T(8,128)(2,1)S(1)} %collective-permute-done.1.refs_7_.refs_8_.refs_9_), channel_id=1, source_target_pairs={{0,24},{1,25},{2,26},{3,27},{4,28},{5,29},{6,30},{7,31},{8,0},{9,1... | collective-permute-start | bytes 1966088 | tf_op jit(solution)/shard_map/ppermute | solution.py:27
  31.9 16.2 %collective-permute-start.2 = (bf16[512,640]{1,0:T(8,128)(2,1)S(1)}, bf16[512,640]{1,0:T(8,128)(2,1)S(1)}, u32[]{:S(2)}, u32[]{:S(2)}) collective-permute-start(bf16[512,640]{1,0:T(8,128)(2,1)S(1)} %collective-permute-done.1.refs_7_.refs_8_.refs_9_), channel_id=1, source_target_pairs={{0,8},{1,9},{2,10},{3,11},{4,12},{5,13},{6,14},{7,15},{8,16},{9,17... | collective-permute-start | bytes 1966088 | tf_op jit(solution)/shard_map/ppermute | solution.py:27
  35.0 15.6 %collective-permute-start.8 = (bf16[256,640]{1,0:T(8,128)(2,1)S(1)}, bf16[256,640]{1,0:T(8,128)(2,1)S(1)}, u32[]{:S(2)}, u32[]{:S(2)}) collective-permute-start(bf16[256,640]{1,0:T(8,128)(2,1)S(1)} %get-tuple-element.32.refs_0_), channel_id=1, source_target_pairs={{0,2},{1,3},{2,4},{3,5},{4,6},{5,7},{6,0},{7,1},{8,10},{9,11},{10,... | collective-permute-start | bytes 983048 | tf_op jit(solution)/shard_map/ppermute | solution.py:27
  35.9 6.9 %copy-start.2 = (bf16[512,640]{1,0:T(8,128)(2,1)}, bf16[512,640]{1,0:T(8,128)(2,1)S(1)}, u32[]{:S(2)}) copy-start(bf16[512,640]{1,0:T(8,128)(2,1)S(1)} %collective-permute-done.4.refs_3_.refs_4_.refs_5_) | copy-start | bytes 1966084
  35.9 14.7 %collective-permute-start.9 = (bf16[256,640]{1,0:T(8,128)(2,1)S(1)}, bf16[256,640]{1,0:T(8,128)(2,1)S(1)}, u32[]{:S(2)}, u32[]{:S(2)}) collective-permute-start(bf16[256,640]{1,0:T(8,128)(2,1)S(1)} %get-tuple-element.32.refs_0_), channel_id=1, source_target_pairs={{0,6},{1,7},{2,0},{3,1},{4,2},{5,3},{6,4},{7,5},{8,14},{9,15},{10,... | collective-permute-start | bytes 983048 | tf_op jit(solution)/shard_map/ppermute | solution.py:27
  38.3 4.5 %copy-start.4 = (bf16[512,640]{1,0:T(8,128)(2,1)}, bf16[512,640]{1,0:T(8,128)(2,1)S(1)}, u32[]{:S(2)}) copy-start(bf16[512,640]{1,0:T(8,128)(2,1)S(1)} %collective-permute-done.6.refs_5_.refs_6_.refs_7_) | copy-start | bytes 1966084
  38.3 19.7 %collective-permute-start = (bf16[256,640]{1,0:T(8,128)(2,1)S(1)}, bf16[256,640]{1,0:T(8,128)(2,1)S(1)}, u32[]{:S(2)}, u32[]{:S(2)}) collective-permute-start(bf16[256,640]{1,0:T(8,128)(2,1)S(1)} %get-tuple-element.32.refs_0_), channel_id=1, source_target_pairs={{0,4},{1,5},{2,6},{3,7},{4,0},{5,1},{6,2},{7,3},{8,12},{9,13},{10,... | collective-permute-start | bytes 983048 | tf_op jit(solution)/shard_map/ppermute | solution.py:27
  42.8 2.3 %slice-start.1 = ((bf16[512,640]{1,0:T(8,128)(2,1)}), bf16[256,640]{1,0:T(8,128)(2,1)S(1)}, s32[]{:S(2)}) async-start(bf16[512,640]{1,0:T(8,128)(2,1)} %copy-done.4), calls=%async_computation.3 | async-start | bytes 655360 | tf_op jit(solution)/shard_map/slice | solution.py:437
  42.8 5.3 %slice-start = ((bf16[512,640]{1,0:T(8,128)(2,1)}), bf16[256,640]{1,0:T(8,128)(2,1)S(1)}, s32[]{:S(2)}) async-start(bf16[512,640]{1,0:T(8,128)(2,1)} %copy-done.2), calls=%async_computation.2 | async-start | bytes 655360 | tf_op jit(solution)/shard_map/slice | solution.py:436
  45.1 5.5 %copy-start.3 = (bf16[512,640]{1,0:T(8,128)(2,1)S(1)}, bf16[512,640]{1,0:T(8,128)(2,1)}, u32[]{:S(2)}) copy-start(bf16[512,640]{1,0:T(8,128)(2,1)} %copy-done.2) | copy-start | bytes 1966084
  45.1 5.5 %copy-start.5 = (bf16[512,640]{1,0:T(8,128)(2,1)S(1)}, bf16[512,640]{1,0:T(8,128)(2,1)}, u32[]{:S(2)}) copy-start(bf16[512,640]{1,0:T(8,128)(2,1)} %copy-done.4) | copy-start | bytes 1966084
  45.2 5.5 %copy-start.9 = (bf16[512,640]{1,0:T(8,128)(2,1)S(1)}, bf16[512,640]{1,0:T(8,128)(2,1)}, u32[]{:S(2)}) copy-start(bf16[512,640]{1,0:T(8,128)(2,1)} %get-tuple-element.33.refs_2_.refs_3_.refs_1_) | copy-start | bytes 1966084
  45.2 16.2 %collective-permute-start.7 = (bf16[512,640]{1,0:T(8,128)(2,1)S(1)}, bf16[512,640]{1,0:T(8,128)(2,1)S(1)}, u32[]{:S(2)}, u32[]{:S(2)}) collective-permute-start(bf16[512,640]{1,0:T(8,128)(2,1)S(1)} %pad_maximum_fusion.1), channel_id=1, source_target_pairs={{0,24},{1,25},{2,26},{3,27},{4,28},{5,29},{6,30},{7,31},{8,0},{9,1... | collective-permute-start | bytes 1966088 | tf_op jit(solution)/shard_map/ppermute | solution.py:27
  48.1 15.0 %collective-permute-start.5 = (bf16[512,640]{1,0:T(8,128)(2,1)S(1)}, bf16[512,640]{1,0:T(8,128)(2,1)S(1)}, u32[]{:S(2)}, u32[]{:S(2)}) collective-permute-start(bf16[512,640]{1,0:T(8,128)(2,1)S(1)} %pad_maximum_fusion), channel_id=1, source_target_pairs={{0,8},{1,9},{2,10},{3,11},{4,12},{5,13},{6,14},{7,15},{8,16},{9,17... | collective-permute-start | bytes 1966088 | tf_op jit(solution)/shard_map/ppermute | solution.py:27
  67.0 20.1 %collective-permute-start.10 = (bf16[304,640]{1,0:T(8,128)(2,1)S(1)}, bf16[304,640]{1,0:T(8,128)(2,1)S(1)}, u32[]{:S(2)}, u32[]{:S(2)}) collective-permute-start(bf16[304,640]{1,0:T(8,128)(2,1)S(1)} %far_across.1.refs_13_), channel_id=1, source_target_pairs={{0,4},{1,5},{2,6},{3,7},{4,0},{5,1},{6,2},{7,3},{8,12},{9,13},{10,... | collective-permute-start | bytes 1167368 | tf_op jit(solution)/shard_map/ppermute | solution.py:27
  76.4 7.6 %collective-permute-start.11 = (bf16[288,640]{1,0:T(8,128)(2,1)S(1)}, bf16[288,640]{1,0:T(8,128)(2,1)S(1)}, u32[]{:S(2)}, u32[]{:S(2)}) collective-permute-start(bf16[288,640]{1,0:T(8,128)(2,1)S(1)} %get-tuple-element.43.refs_12_), channel_id=1, source_target_pairs={{0,6},{1,7},{2,0},{3,1},{4,2},{5,3},{6,4},{7,5},{8,14},{9,15},{10,... | collective-permute-start | bytes 1105928 | tf_op jit(solution)/shard_map/ppermute | solution.py:27
  78.3 8.7 %collective-permute-start.12 = (bf16[288,640]{1,0:T(8,128)(2,1)S(1)}, bf16[288,640]{1,0:T(8,128)(2,1)S(1)}, u32[]{:S(2)}, u32[]{:S(2)}) collective-permute-start(bf16[288,640]{1,0:T(8,128)(2,1)S(1)} %get-tuple-element.44), channel_id=1, source_target_pairs={{0,2},{1,3},{2,4},{3,5},{4,6},{5,7},{6,0},{7,1},{8,10},{9,11},{10,... | collective-permute-start | bytes 1105928 | tf_op jit(solution)/shard_map/ppermute | solution.py:27
  78.5 8.5 %copy-start.1 = (bf16[640,1280]{1,0:T(8,128)(2,1)S(1)}, bf16[640,1280]{1,0:T(8,128)(2,1)}, u32[]{:S(2)}) copy-start(bf16[640,1280]{1,0:T(8,128)(2,1)} %w_ref.1) | copy-start | bytes 4915204
  89.5 22.2 %copy-start.6 = (f32[1280]{0:T(1024)S(1)}, f32[1280]{0:T(1024)}, u32[]{:S(2)}) copy-start(f32[1280]{0:T(1024)} %gain_ref.3) | copy-start | bytes 15364
  89.5 22.2 %copy-start.8 = (f32[640]{0:T(1024)S(1)}, f32[640]{0:T(1024)}, u32[]{:S(2)}) copy-start(f32[640]{0:T(1024)} %shift_ref.1) | copy-start | bytes 7684
  89.6 22.1 %collective-permute-start.13 = (f32[64,1280]{1,0:T(8,128)S(1)}, f32[64,1280]{1,0:T(8,128)S(1)}, u32[]{:S(2)}, u32[]{:S(2)}) collective-permute-start(f32[64,1280]{1,0:T(8,128)S(1)} %get-tuple-element.54), channel_id=1, source_target_pairs={{0,1},{1,2},{2,3},{3,4},{4,5},{5,6},{6,7},{7,8},{8,9},{9,10},{10,1... | collective-permute-start | bytes 983048 | tf_op jit(solution)/shard_map/ppermute | solution.py:460
  94.0 17.8 %collective-permute-start.14 = (f32[64,1280]{1,0:T(8,128)S(1)}, f32[64,1280]{1,0:T(8,128)S(1)}, u32[]{:S(2)}, u32[]{:S(2)}) collective-permute-start(f32[64,1280]{1,0:T(8,128)S(1)} %get-tuple-element.53), channel_id=1, source_target_pairs={{1,0},{2,1},{3,2},{4,3},{5,4},{6,5},{7,6},{8,7},{9,8},{10,9},{11,1... | collective-permute-start | bytes 983048 | tf_op jit(solution)/shard_map/ppermute | solution.py:461

commit v3 on v2

--- a/solution.py
+++ b/solution.py
@@ -36,16 +36,20 @@
     return jnp.where(inside, 1.0, 0.0).astype(BF)
 
 
+def exact_dots(rows, ones):
+    at = lax.broadcasted_iota(jnp.int32, (16, rows[0].shape[1]), 0)
+    cut = jnp.zeros(at.shape, F32)
+    for i, rest in enumerate(rows):
+        for piece in range(3):
+            part = rest.astype(BF).astype(F32)
+            rest = rest - part
+            cut = jnp.where(at == 8 * i + piece, part, cut)
+    found = jnp.dot(cut.astype(BF), ones, preferred_element_type=F32)
+    return [jnp.sum(found[8 * i : 8 * i + 8], axis=0, keepdims=True) for i in range(len(rows))]
+
+
 def exact_dot(row, ones):
-    at = lax.broadcasted_iota(jnp.int32, (16, row.shape[1]), 0)
-    rest, cut = row, jnp.zeros((16, row.shape[1]), F32)
-    for piece in range(3):
-        part = rest.astype(BF).astype(F32)
-        rest = rest - part
-        cut = jnp.where(at == piece, part, cut)
-    return jnp.sum(
-        jnp.dot(cut.astype(BF), ones, preferred_element_type=F32), axis=0, keepdims=True
-    )
+    return exact_dots([row], ones)[0]
 
 
 def group_matrices(channels):
@@ -72,9 +76,11 @@
     total = jnp.sum(stats, axis=0, keepdims=True)
     mean = total / peers
     between = jnp.sum(jnp.square(stats - mean), axis=0, keepdims=True) * count
-    lead = members_of(channels, False, 0)
-    center = exact_dot(mean, lead)
-    spread = exact_dot(between, lead) + exact_dot(total, members_of(channels, False, GROUPS))
+    lane = lax.broadcasted_iota(jnp.int32, mean.shape, 1)
+    both = members_of(channels, False, 0) + members_of(channels, False, GROUPS)
+    center, spread = exact_dots(
+        [jnp.where(lane < GROUPS, mean, 0.0), jnp.where(lane < GROUPS, between, total)], both
+    )
     return center, lax.rsqrt(spread / (count * peers) + EPS)
 
 

time: 118 us -> 118 us (level)
  no operation moved by 1% of the time
where the time goes in v3:
time: 118 us
  Pallas kernels  46.7 us (40%)
  blocking collectives  35.5 us (30%)
  starting transfers between devices  24.6 us (21%)
  waiting for transfers between devices  9.62 us (8%)
    all_to_all x2, blocking collectives, everyones(): return lax.all_to_all(stats, 'patch', 0, 0, tiled=True)  35.5 us
    pallas_call x6, Pallas kernels, attend(): pl.pallas_call(functools.partial(attend_kernel, plan, bool(state), final,...  31.7 us
    ppermute x13, starting transfers between devices, shifted(): return lax.ppermute(x, 'patch', pairs)  18.9 us
    ppermute x13, waiting for transfers between devices, shifted(): return lax.ppermute(x, 'patch', pairs)  9.61 us
    pallas_call x1, Pallas kernels, convolve(): pl.pallas_call(conv_kernel, in_specs=[VMEM] * 7, out_specs=VMEM, out_shap...  6.05 us
    ppermute x1, starting transfers between devices, shards(): above = lax.ppermute(hidden[tok_count - col_count:], 'patch', down)  4.34 us
    pallas_call x1, Pallas kernels, norm_stats(): pl.pallas_call(stats_kernel, in_specs=[HBM] * 6, out_specs=[VMEM] * 5, ou...  3.77 us
    pallas_call x1, Pallas kernels, project(): pl.pallas_call(project_kernel, in_specs=[VMEM] * 6, out_specs=[VMEM] * 4,...  2.71 us
  transfers between devices with their start and end apart: 15, of which 4 were waited for; matrix products, arithmetic and copies ran while one was open for 0% of the time, Pallas kernels for 26%

profile of v3, /device:TPU:0, one launch (start us, length us, event | category | flops | bytes accessed | tf_op | source)
XLA Modules:
  0.0 117.6 jit_solution(7036956797948477076)
XLA Ops:
  0.7 3.8 %norm_stats.1 = (f32[32,128]{1,0:T(8,128)}, bf16[512,640]{1,0:T(8,128)(2,1)}, bf16[1280,640]{1,0:T(8,128)(2,1)S(1)}, bf16[1280,640]{1,0:T(8,128)(2,1)S(1)}, bf16[1280,640]{1,0:T(8,128)(2,1)S(1)}) custom-call(bf16[256,1280]{1,0:T(8,128)(2,1)} %bitcast.10, bf16[256,640]{1,0:T(8,128)(2,1)} %k_ref.1, bf16[256,640]{1,0:T(8,128)(2,1)} %v_ref.1, ...), custom_call_target="tpu_custom_call" | custom-call | flops 1310720 | bytes 655360 | tf_op jit(solution)/shard_map/norm_stats/pallas_call | solution.py:124
  4.4 3.2 %collective-permute-start.1 = (bf16[512,640]{1,0:T(8,128)(2,1)}, bf16[512,640]{1,0:T(8,128)(2,1)S(1)}, u32[]{:S(2)}, u32[]{:S(2)}) collective-permute-start(bf16[512,640]{1,0:T(8,128)(2,1)} %get-tuple-element.33.refs_2_.refs_3_.refs_1_), channel_id=1, source_target_pairs={{0,1},{1,0},{2,3},{3,2},{4,5},{5,4},{6,7},{7,6},{8,9},{9,8},{10,11... | collective-permute-start | bytes 1966088 | tf_op jit(solution)/shard_map/ppermute | solution.py:27
  7.6 1.6 %collective-permute-start.4 = (bf16[512,640]{1,0:T(8,128)(2,1)}, bf16[512,640]{1,0:T(8,128)(2,1)S(1)}, u32[]{:S(2)}, u32[]{:S(2)}) collective-permute-start(bf16[512,640]{1,0:T(8,128)(2,1)} %get-tuple-element.33.refs_2_.refs_3_.refs_1_), channel_id=1, source_target_pairs={{0,8},{1,9},{2,10},{3,11},{4,12},{5,13},{6,14},{7,15},{8,16},{9,17... | collective-permute-start | bytes 1966088 | tf_op jit(solution)/shard_map/ppermute | solution.py:27
  9.2 1.7 %collective-permute-start.6 = (bf16[512,640]{1,0:T(8,128)(2,1)}, bf16[512,640]{1,0:T(8,128)(2,1)S(1)}, u32[]{:S(2)}, u32[]{:S(2)}) collective-permute-start(bf16[512,640]{1,0:T(8,128)(2,1)} %get-tuple-element.33.refs_2_.refs_3_.refs_1_), channel_id=1, source_target_pairs={{0,24},{1,25},{2,26},{3,27},{4,28},{5,29},{6,30},{7,31},{8,0},{9,1... | collective-permute-start | bytes 1966088 | tf_op jit(solution)/shard_map/ppermute | solution.py:27
  10.9 19.2 %all_to_all.22 = f32[32,1,128]{2,1,0:T(1,128)S(1)} all-to-all(f32[32,1,128]{2,1,0:T(1,128)} %bitcast.17), channel_id=1, replica_groups=mesh['batch'=4,'patch'=32] {'patch'}, dimensions={0} | all-to-all | bytes 32768 | tf_op jit(solution)/shard_map/all_to_all | solution.py:410
  30.1 0.0 collective-permute-done.1.refs_7_.refs_8_.refs_9_
  30.1 1.8 %collective-permute-start.3 = (bf16[512,640]{1,0:T(8,128)(2,1)S(1)}, bf16[512,640]{1,0:T(8,128)(2,1)S(1)}, u32[]{:S(2)}, u32[]{:S(2)}) collective-permute-start(bf16[512,640]{1,0:T(8,128)(2,1)S(1)} %collective-permute-done.1.refs_7_.refs_8_.refs_9_), channel_id=1, source_target_pairs={{0,24},{1,25},{2,26},{3,27},{4,28},{5,29},{6,30},{7,31},{8,0},{9,1... | collective-permute-start | bytes 1966088 | tf_op jit(solution)/shard_map/ppermute | solution.py:27
  31.9 0.2 collective-permute-start.2
  32.1 0.0 copy-done
  32.1 2.7 %project.1 = (bf16[256,640]{1,0:T(8,128)(2,1)S(1)}, bf16[256,640]{1,0:T(8,128)(2,1)}, bf16[256,640]{1,0:T(8,128)(2,1)}, bf16[512,640]{1,0:T(8,128)(2,1)S(1)}) custom-call(f32[32,128]{1,0:T(8,128)S(1)} %bitcast.13, bf16[256,1280]{1,0:T(8,128)(2,1)S(1)} %bitcast.11, f32[1280]{0:T(1024)S(1)} %copy-done.7, bf16[1280,640]{1,0:T(8,128)(2,1)S(1)} %get-tuple-element.29.wq, ...), custom_call_target="tpu_custom_call" | custom-call | flops 1258291200 | bytes 4915200 | tf_op jit(solution)/shard_map/project/pallas_call | solution.py:155
  34.8 0.8 collective-permute-start.8
  35.7 0.0 collective-permute-done.4.refs_3_.refs_4_.refs_5_
  35.7 2.4 %collective-permute-start.9 = (bf16[256,640]{1,0:T(8,128)(2,1)S(1)}, bf16[256,640]{1,0:T(8,128)(2,1)S(1)}, u32[]{:S(2)}, u32[]{:S(2)}) collective-permute-start(bf16[256,640]{1,0:T(8,128)(2,1)S(1)} %get-tuple-element.32.refs_0_), channel_id=1, source_target_pairs={{0,6},{1,7},{2,0},{3,1},{4,2},{5,3},{6,4},{7,5},{8,14},{9,15},{10,... | collective-permute-start | bytes 983048 | tf_op jit(solution)/shard_map/ppermute | solution.py:27
  38.1 0.0 collective-permute-done.6.refs_5_.refs_6_.refs_7_
  38.1 0.2 collective-permute-start
  38.3 4.2 %near_own.1 = (f32[256,640]{1,0:T(8,128)S(1)}, f32[256,640]{1,0:T(8,128)S(1)}, f32[256,640]{1,0:T(8,128)S(1)}) custom-call(bf16[256,640]{1,0:T(8,128)(2,1)S(1)} %get-tuple-element.32.refs_0_, bf16[512,640]{1,0:T(8,128)(2,1)S(1)} %get-tuple-element.35.refs_1_.refs_2_, bf16[512,640]{1,0:T(8,128)(2,1)S(1)} %get-tuple-element.35.refs_1_.refs_2_, ...), custom_call_target="tpu_custom_call" | custom-call | flops 2684354560 | bytes 524288 | tf_op jit(solution)/shard_map/near_own/pallas_call | solution.py:297
  42.6 0.0 slice-start.1
  42.6 0.0 slice-start
  42.6 2.4 %collective-permute-done.3.refs_3_.refs_4_.refs_5_ = bf16[512,640]{1,0:T(8,128)(2,1)S(1)} collective-permute-done((bf16[512,640]{1,0:T(8,128)(2,1)S(1)}, bf16[512,640]{1,0:T(8,128)(2,1)S(1)}, u32[]{:S(2)}, u32[]{:S(2)}) %collective-permute-start.3) | collective-permute-done | bytes 655392 | tf_op jit(solution)/shard_map/ppermute | solution.py:27
  45.1 0.1 pad_maximum_fusion.1
  45.2 2.9 %collective-permute-start.7 = (bf16[512,640]{1,0:T(8,128)(2,1)S(1)}, bf16[512,640]{1,0:T(8,128)(2,1)S(1)}, u32[]{:S(2)}, u32[]{:S(2)}) collective-permute-start(bf16[512,640]{1,0:T(8,128)(2,1)S(1)} %pad_maximum_fusion.1), channel_id=1, source_target_pairs={{0,24},{1,25},{2,26},{3,27},{4,28},{5,29},{6,30},{7,31},{8,0},{9,1... | collective-permute-start | bytes 1966088 | tf_op jit(solution)/shard_map/ppermute | solution.py:27
  48.0 0.0 collective-permute-done.2.refs_1_.refs_2_.refs_3_
  48.1 0.1 pad_maximum_fusion
  48.1 0.3 collective-permute-start.5
  48.4 2.0 %collective-permute-done.8.refs_0_ = bf16[256,640]{1,0:T(8,128)(2,1)S(1)} collective-permute-done((bf16[256,640]{1,0:T(8,128)(2,1)S(1)}, bf16[256,640]{1,0:T(8,128)(2,1)S(1)}, u32[]{:S(2)}, u32[]{:S(2)}) %collective-permute-start.8) | collective-permute-done | bytes 327712 | tf_op jit(solution)/shard_map/ppermute | solution.py:27
  50.4 0.0 collective-permute-done.9.refs_1_
  50.4 7.3 %near_beside.1 = (f32[512,640]{1,0:T(8,128)S(1)}, f32[512,640]{1,0:T(8,128)S(1)}, f32[512,640]{1,0:T(8,128)S(1)}) custom-call(bf16[256,640]{1,0:T(8,128)(2,1)S(1)} %collective-permute-done.8.refs_0_, bf16[256,640]{1,0:T(8,128)(2,1)S(1)} %collective-permute-done.9.refs_1_, bf16[512,640]{1,0:T(8,128)(2,1)S(1)} %copy-done.9, bf16[512,640]{1,0:T(8,128)(2,1)S(1)} %copy-done.9, ...), custom_call_target="tpu_custom_call" | custom-call | flops 5368709120 | bytes 524288 | tf_op jit(solution)/shard_map/near_beside/pallas_call | solution.py:297
  57.7 0.0 collective-permute-done.refs_0_
  57.7 3.4 %near_across.1 = (f32[256,640]{1,0:T(8,128)S(1)}, f32[256,640]{1,0:T(8,128)S(1)}, f32[256,640]{1,0:T(8,128)S(1)}) custom-call(bf16[256,640]{1,0:T(8,128)(2,1)S(1)} %collective-permute-done.refs_0_, bf16[512,640]{1,0:T(8,128)(2,1)S(1)} %copy-done.9, bf16[512,640]{1,0:T(8,128)(2,1)S(1)} %copy-done.9, bf16[512,640]{1,0:T(8,128)(2,1)S(1)} %copy-done.3, ...), custom_call_target="tpu_custom_call" | custom-call | flops 2684354560 | bytes 524288 | tf_op jit(solution)/shard_map/near_across/pallas_call | solution.py:297
  61.2 0.0 collective-permute-done.7.refs_6_.refs_8_.refs_7_.refs_9_
  61.2 1.9 %collective-permute-done.5.refs_5_.refs_7_.refs_6_.refs_8_ = bf16[512,640]{1,0:T(8,128)(2,1)S(1)} collective-permute-done((bf16[512,640]{1,0:T(8,128)(2,1)S(1)}, bf16[512,640]{1,0:T(8,128)(2,1)S(1)}, u32[]{:S(2)}, u32[]{:S(2)}) %collective-permute-start.5) | collective-permute-done | bytes 655392 | tf_op jit(solution)/shard_map/ppermute | solution.py:27
  63.1 3.8 %far_across.1.refs_13_ = bf16[304,640]{1,0:T(8,128)(2,1)S(1)} custom-call(bf16[256,640]{1,0:T(8,128)(2,1)S(1)} %collective-permute-done.refs_0_, bf16[512,640]{1,0:T(8,128)(2,1)S(1)} %collective-permute-done.2.refs_1_.refs_2_.refs_3_, bf16[512,640]{1,0:T(8,128)(2,1)S(1)} %collective-permute-done.2.refs_1_.refs_2_.refs_3_, ...), custom_call_target="tpu_custom_call" | custom-call | flops 2684354560 | bytes 524288 | tf_op jit(solution)/shard_map/far_across/pallas_call | solution.py:297
  67.0 1.8 %collective-permute-start.10 = (bf16[304,640]{1,0:T(8,128)(2,1)S(1)}, bf16[304,640]{1,0:T(8,128)(2,1)S(1)}, u32[]{:S(2)}, u32[]{:S(2)}) collective-permute-start(bf16[304,640]{1,0:T(8,128)(2,1)S(1)} %far_across.1.refs_13_), channel_id=1, source_target_pairs={{0,4},{1,5},{2,6},{3,7},{4,0},{5,1},{6,2},{7,3},{8,12},{9,13},{10,... | collective-permute-start | bytes 1167368 | tf_op jit(solution)/shard_map/ppermute | solution.py:27
  68.8 7.5 %far_beside.1 = (bf16[288,640]{1,0:T(8,128)(2,1)S(1)}, bf16[288,640]{1,0:T(8,128)(2,1)S(1)}) custom-call(bf16[256,640]{1,0:T(8,128)(2,1)S(1)} %collective-permute-done.8.refs_0_, bf16[256,640]{1,0:T(8,128)(2,1)S(1)} %collective-permute-done.9.refs_1_, bf16[512,640]{1,0:T(8,128)(2,1)S(1)} %collective-permute-done.2.refs_1_.refs_2_.refs_3_, ...), custom_call_target="tpu_custom_call" | custom-call | flops 335544320 | bytes 32768 | tf_op jit(solution)/shard_map/far_beside/pallas_call | solution.py:297
  76.2 2.1 %collective-permute-start.11 = (bf16[288,640]{1,0:T(8,128)(2,1)S(1)}, bf16[288,640]{1,0:T(8,128)(2,1)S(1)}, u32[]{:S(2)}, u32[]{:S(2)}) collective-permute-start(bf16[288,640]{1,0:T(8,128)(2,1)S(1)} %get-tuple-element.43.refs_12_), channel_id=1, source_target_pairs={{0,6},{1,7},{2,0},{3,1},{4,2},{5,3},{6,4},{7,5},{8,14},{9,15},{10,... | collective-permute-start | bytes 1105928 | tf_op jit(solution)/shard_map/ppermute | solution.py:27
  78.3 0.0 collective-permute-start.12
  78.3 5.5 %far_own.1 = (bf16[288,640]{1,0:T(8,128)(2,1)S(1)}, bf16[9,1280,640]{2,1,0:T(8,128)(2,1)S(1)}) custom-call(bf16[256,640]{1,0:T(8,128)(2,1)S(1)} %get-tuple-element.32.refs_0_, bf16[512,640]{1,0:T(8,128)(2,1)S(1)} %collective-permute-done.2.refs_1_.refs_2_.refs_3_, bf16[512,640]{1,0:T(8,128)(2,1)S(1)} %collective-permute-done.2.refs_1_.refs_2_.refs_3_, ...), custom_call_target="tpu_custom_call" | custom-call | flops 167772160 | bytes 32768 | tf_op jit(solution)/shard_map/far_own/pallas_call | solution.py:297
  83.8 0.0 collective-permute-done.11.p1
  83.8 3.2 %collective-permute-done.12.p2 = bf16[288,640]{1,0:T(8,128)(2,1)S(1)} collective-permute-done((bf16[288,640]{1,0:T(8,128)(2,1)S(1)}, bf16[288,640]{1,0:T(8,128)(2,1)S(1)}, u32[]{:S(2)}, u32[]{:S(2)}) %collective-permute-start.12) | collective-permute-done | bytes 368672 | tf_op jit(solution)/shard_map/ppermute | solution.py:27
  87.0 0.0 collective-permute-done.10.p0
  87.0 2.5 %merge_project.1 = (f32[256,1280]{1,0:T(8,128)S(1)}, f32[32,128]{1,0:T(8,128)S(1)}) custom-call(bf16[304,640]{1,0:T(8,128)(2,1)S(1)} %collective-permute-done.10.p0, bf16[288,640]{1,0:T(8,128)(2,1)S(1)} %collective-permute-done.11.p1, bf16[288,640]{1,0:T(8,128)(2,1)S(1)} %collective-permute-done.12.p2, bf16[288,640]{1,0:T(8,128)(2,1)S(1)} %get-tuple-element.47.p3, ...), custom_call_target="tpu_custom_call" | custom-call | flops 419430400 | bytes 1638400 | tf_op jit(solution)/shard_map/merge_project/pallas_call | solution.py:347
  89.5 0.0 copy-start.8
  89.6 4.3 %collective-permute-start.13 = (f32[64,1280]{1,0:T(8,128)S(1)}, f32[64,1280]{1,0:T(8,128)S(1)}, u32[]{:S(2)}, u32[]{:S(2)}) collective-permute-start(f32[64,1280]{1,0:T(8,128)S(1)} %get-tuple-element.54), channel_id=1, source_target_pairs={{0,1},{1,2},{2,3},{3,4},{4,5},{5,6},{6,7},{7,8},{8,9},{9,10},{10,1... | collective-permute-start | bytes 983048 | tf_op jit(solution)/shard_map/ppermute | solution.py:466
  93.9 1.3 %collective-permute-start.14 = (f32[64,1280]{1,0:T(8,128)S(1)}, f32[64,1280]{1,0:T(8,128)S(1)}, u32[]{:S(2)}, u32[]{:S(2)}) collective-permute-start(f32[64,1280]{1,0:T(8,128)S(1)} %get-tuple-element.53), channel_id=1, source_target_pairs={{1,0},{2,1},{3,2},{4,3},{5,4},{6,5},{7,6},{8,7},{9,8},{10,9},{11,1... | collective-permute-start | bytes 983048 | tf_op jit(solution)/shard_map/ppermute | solution.py:467
  95.2 16.3 %all_to_all.23 = f32[32,1,128]{2,1,0:T(1,128)S(1)} all-to-all(f32[32,1,128]{2,1,0:T(1,128)S(1)} %bitcast.15), channel_id=1, replica_groups=mesh['batch'=4,'patch'=32] {'patch'}, dimensions={0} | all-to-all | bytes 32768 | tf_op jit(solution)/shard_map/all_to_all | solution.py:410
  111.5 0.0 collective-permute-done.13.above_ref
  111.5 0.0 collective-permute-done.14.below_ref
  111.5 6.0 %norm_convolve.1 = bf16[256,640]{1,0:T(8,128)(2,1)} custom-call(f32[32,128]{1,0:T(8,128)S(1)} %bitcast.14, f32[256,1280]{1,0:T(8,128)S(1)} %get-tuple-element.49.hidden_ref, f32[64,1280]{1,0:T(8,128)S(1)} %collective-permute-done.13.above_ref, f32[64,1280]{1,0:T(8,128)S(1)} %collective-permute-done.14.below_ref, f32[1280]{0:T(1024)S(1)} %copy-done.6, ...), custom_call_target="tpu_custom_call" | custom-call | flops 3774873600 | bytes 14745600 | tf_op jit(solution)/shard_map/norm_convolve/pallas_call | solution.py:395
  (23 shorter events, 0.1 us)
Async XLA Ops:
  0.6 31.5 %copy-start = (bf16[4,64,1280]{2,1,0:T(8,128)(2,1)S(1)}, bf16[4,64,1280]{2,1,0:T(8,128)(2,1)}, u32[]{:S(2)}) copy-start(bf16[4,64,1280]{2,1,0:T(8,128)(2,1)} %param.11) | copy-start | bytes 1966084
  0.6 31.5 %copy-start.7 = (f32[1280]{0:T(1024)S(1)}, f32[1280]{0:T(1024)}, u32[]{:S(2)}) copy-start(f32[1280]{0:T(1024)} %gain_ref.2) | copy-start | bytes 15364
  4.4 25.7 %collective-permute-start.1 = (bf16[512,640]{1,0:T(8,128)(2,1)}, bf16[512,640]{1,0:T(8,128)(2,1)S(1)}, u32[]{:S(2)}, u32[]{:S(2)}) collective-permute-start(bf16[512,640]{1,0:T(8,128)(2,1)} %get-tuple-element.33.refs_2_.refs_3_.refs_1_), channel_id=1, source_target_pairs={{0,1},{1,0},{2,3},{3,2},{4,5},{5,4},{6,7},{7,6},{8,9},{9,8},{10,11... | collective-permute-start | bytes 1966088 | tf_op jit(solution)/shard_map/ppermute | solution.py:27
  7.6 28.1 %collective-permute-start.4 = (bf16[512,640]{1,0:T(8,128)(2,1)}, bf16[512,640]{1,0:T(8,128)(2,1)S(1)}, u32[]{:S(2)}, u32[]{:S(2)}) collective-permute-start(bf16[512,640]{1,0:T(8,128)(2,1)} %get-tuple-element.33.refs_2_.refs_3_.refs_1_), channel_id=1, source_target_pairs={{0,8},{1,9},{2,10},{3,11},{4,12},{5,13},{6,14},{7,15},{8,16},{9,17... | collective-permute-start | bytes 1966088 | tf_op jit(solution)/shard_map/ppermute | solution.py:27
  9.2 28.9 %collective-permute-start.6 = (bf16[512,640]{1,0:T(8,128)(2,1)}, bf16[512,640]{1,0:T(8,128)(2,1)S(1)}, u32[]{:S(2)}, u32[]{:S(2)}) collective-permute-start(bf16[512,640]{1,0:T(8,128)(2,1)} %get-tuple-element.33.refs_2_.refs_3_.refs_1_), channel_id=1, source_target_pairs={{0,24},{1,25},{2,26},{3,27},{4,28},{5,29},{6,30},{7,31},{8,0},{9,1... | collective-permute-start | bytes 1966088 | tf_op jit(solution)/shard_map/ppermute | solution.py:27
  30.1 14.9 %collective-permute-start.3 = (bf16[512,640]{1,0:T(8,128)(2,1)S(1)}, bf16[512,640]{1,0:T(8,128)(2,1)S(1)}, u32[]{:S(2)}, u32[]{:S(2)}) collective-permute-start(bf16[512,640]{1,0:T(8,128)(2,1)S(1)} %collective-permute-done.1.refs_7_.refs_8_.refs_9_), channel_id=1, source_target_pairs={{0,24},{1,25},{2,26},{3,27},{4,28},{5,29},{6,30},{7,31},{8,0},{9,1... | collective-permute-start | bytes 1966088 | tf_op jit(solution)/shard_map/ppermute | solution.py:27
  31.9 16.2 %collective-permute-start.2 = (bf16[512,640]{1,0:T(8,128)(2,1)S(1)}, bf16[512,640]{1,0:T(8,128)(2,1)S(1)}, u32[]{:S(2)}, u32[]{:S(2)}) collective-permute-start(bf16[512,640]{1,0:T(8,128)(2,1)S(1)} %collective-permute-done.1.refs_7_.refs_8_.refs_9_), channel_id=1, source_target_pairs={{0,8},{1,9},{2,10},{3,11},{4,12},{5,13},{6,14},{7,15},{8,16},{9,17... | collective-permute-start | bytes 1966088 | tf_op jit(solution)/shard_map/ppermute | solution.py:27
  34.8 15.6 %collective-permute-start.8 = (bf16[256,640]{1,0:T(8,128)(2,1)S(1)}, bf16[256,640]{1,0:T(8,128)(2,1)S(1)}, u32[]{:S(2)}, u32[]{:S(2)}) collective-permute-start(bf16[256,640]{1,0:T(8,128)(2,1)S(1)} %get-tuple-element.32.refs_0_), channel_id=1, source_target_pairs={{0,2},{1,3},{2,4},{3,5},{4,6},{5,7},{6,0},{7,1},{8,10},{9,11},{10,... | collective-permute-start | bytes 983048 | tf_op jit(solution)/shard_map/ppermute | solution.py:27
  35.7 6.9 %copy-start.2 = (bf16[512,640]{1,0:T(8,128)(2,1)}, bf16[512,640]{1,0:T(8,128)(2,1)S(1)}, u32[]{:S(2)}) copy-start(bf16[512,640]{1,0:T(8,128)(2,1)S(1)} %collective-permute-done.4.refs_3_.refs_4_.refs_5_) | copy-start | bytes 1966084
  35.7 14.7 %collective-permute-start.9 = (bf16[256,640]{1,0:T(8,128)(2,1)S(1)}, bf16[256,640]{1,0:T(8,128)(2,1)S(1)}, u32[]{:S(2)}, u32[]{:S(2)}) collective-permute-start(bf16[256,640]{1,0:T(8,128)(2,1)S(1)} %get-tuple-element.32.refs_0_), channel_id=1, source_target_pairs={{0,6},{1,7},{2,0},{3,1},{4,2},{5,3},{6,4},{7,5},{8,14},{9,15},{10,... | collective-permute-start | bytes 983048 | tf_op jit(solution)/shard_map/ppermute | solution.py:27
  38.1 4.5 %copy-start.4 = (bf16[512,640]{1,0:T(8,128)(2,1)}, bf16[512,640]{1,0:T(8,128)(2,1)S(1)}, u32[]{:S(2)}) copy-start(bf16[512,640]{1,0:T(8,128)(2,1)S(1)} %collective-permute-done.6.refs_5_.refs_6_.refs_7_) | copy-start | bytes 1966084
  38.1 19.7 %collective-permute-start = (bf16[256,640]{1,0:T(8,128)(2,1)S(1)}, bf16[256,640]{1,0:T(8,128)(2,1)S(1)}, u32[]{:S(2)}, u32[]{:S(2)}) collective-permute-start(bf16[256,640]{1,0:T(8,128)(2,1)S(1)} %get-tuple-element.32.refs_0_), channel_id=1, source_target_pairs={{0,4},{1,5},{2,6},{3,7},{4,0},{5,1},{6,2},{7,3},{8,12},{9,13},{10,... | collective-permute-start | bytes 983048 | tf_op jit(solution)/shard_map/ppermute | solution.py:27
  42.6 2.5 %slice-start.1 = ((bf16[512,640]{1,0:T(8,128)(2,1)}), bf16[256,640]{1,0:T(8,128)(2,1)S(1)}, s32[]{:S(2)}) async-start(bf16[512,640]{1,0:T(8,128)(2,1)} %copy-done.4), calls=%async_computation.3 | async-start | bytes 655360 | tf_op jit(solution)/shard_map/slice | solution.py:443
  42.6 5.5 %slice-start = ((bf16[512,640]{1,0:T(8,128)(2,1)}), bf16[256,640]{1,0:T(8,128)(2,1)S(1)}, s32[]{:S(2)}) async-start(bf16[512,640]{1,0:T(8,128)(2,1)} %copy-done.2), calls=%async_computation.2 | async-start | bytes 655360 | tf_op jit(solution)/shard_map/slice | solution.py:442
  45.1 5.3 %copy-start.3 = (bf16[512,640]{1,0:T(8,128)(2,1)S(1)}, bf16[512,640]{1,0:T(8,128)(2,1)}, u32[]{:S(2)}) copy-start(bf16[512,640]{1,0:T(8,128)(2,1)} %copy-done.2) | copy-start | bytes 1966084
  45.1 5.3 %copy-start.5 = (bf16[512,640]{1,0:T(8,128)(2,1)S(1)}, bf16[512,640]{1,0:T(8,128)(2,1)}, u32[]{:S(2)}) copy-start(bf16[512,640]{1,0:T(8,128)(2,1)} %copy-done.4) | copy-start | bytes 1966084
  45.2 5.3 %copy-start.9 = (bf16[512,640]{1,0:T(8,128)(2,1)S(1)}, bf16[512,640]{1,0:T(8,128)(2,1)}, u32[]{:S(2)}) copy-start(bf16[512,640]{1,0:T(8,128)(2,1)} %get-tuple-element.33.refs_2_.refs_3_.refs_1_) | copy-start | bytes 1966084
  45.2 16.0 %collective-permute-start.7 = (bf16[512,640]{1,0:T(8,128)(2,1)S(1)}, bf16[512,640]{1,0:T(8,128)(2,1)S(1)}, u32[]{:S(2)}, u32[]{:S(2)}) collective-permute-start(bf16[512,640]{1,0:T(8,128)(2,1)S(1)} %pad_maximum_fusion.1), channel_id=1, source_target_pairs={{0,24},{1,25},{2,26},{3,27},{4,28},{5,29},{6,30},{7,31},{8,0},{9,1... | collective-permute-start | bytes 1966088 | tf_op jit(solution)/shard_map/ppermute | solution.py:27
  48.1 15.0 %collective-permute-start.5 = (bf16[512,640]{1,0:T(8,128)(2,1)S(1)}, bf16[512,640]{1,0:T(8,128)(2,1)S(1)}, u32[]{:S(2)}, u32[]{:S(2)}) collective-permute-start(bf16[512,640]{1,0:T(8,128)(2,1)S(1)} %pad_maximum_fusion), channel_id=1, source_target_pairs={{0,8},{1,9},{2,10},{3,11},{4,12},{5,13},{6,14},{7,15},{8,16},{9,17... | collective-permute-start | bytes 1966088 | tf_op jit(solution)/shard_map/ppermute | solution.py:27
  67.0 20.1 %collective-permute-start.10 = (bf16[304,640]{1,0:T(8,128)(2,1)S(1)}, bf16[304,640]{1,0:T(8,128)(2,1)S(1)}, u32[]{:S(2)}, u32[]{:S(2)}) collective-permute-start(bf16[304,640]{1,0:T(8,128)(2,1)S(1)} %far_across.1.refs_13_), channel_id=1, source_target_pairs={{0,4},{1,5},{2,6},{3,7},{4,0},{5,1},{6,2},{7,3},{8,12},{9,13},{10,... | collective-permute-start | bytes 1167368 | tf_op jit(solution)/shard_map/ppermute | solution.py:27
  76.2 7.6 %collective-permute-start.11 = (bf16[288,640]{1,0:T(8,128)(2,1)S(1)}, bf16[288,640]{1,0:T(8,128)(2,1)S(1)}, u32[]{:S(2)}, u32[]{:S(2)}) collective-permute-start(bf16[288,640]{1,0:T(8,128)(2,1)S(1)} %get-tuple-element.43.refs_12_), channel_id=1, source_target_pairs={{0,6},{1,7},{2,0},{3,1},{4,2},{5,3},{6,4},{7,5},{8,14},{9,15},{10,... | collective-permute-start | bytes 1105928 | tf_op jit(solution)/shard_map/ppermute | solution.py:27
  78.3 8.7 %collective-permute-start.12 = (bf16[288,640]{1,0:T(8,128)(2,1)S(1)}, bf16[288,640]{1,0:T(8,128)(2,1)S(1)}, u32[]{:S(2)}, u32[]{:S(2)}) collective-permute-start(bf16[288,640]{1,0:T(8,128)(2,1)S(1)} %get-tuple-element.44), channel_id=1, source_target_pairs={{0,2},{1,3},{2,4},{3,5},{4,6},{5,7},{6,0},{7,1},{8,10},{9,11},{10,... | collective-permute-start | bytes 1105928 | tf_op jit(solution)/shard_map/ppermute | solution.py:27
  78.3 8.7 %copy-start.1 = (bf16[640,1280]{1,0:T(8,128)(2,1)S(1)}, bf16[640,1280]{1,0:T(8,128)(2,1)}, u32[]{:S(2)}) copy-start(bf16[640,1280]{1,0:T(8,128)(2,1)} %w_ref.1) | copy-start | bytes 4915204
  89.5 22.0 %copy-start.6 = (f32[1280]{0:T(1024)S(1)}, f32[1280]{0:T(1024)}, u32[]{:S(2)}) copy-start(f32[1280]{0:T(1024)} %gain_ref.3) | copy-start | bytes 15364
  89.5 22.0 %copy-start.8 = (f32[640]{0:T(1024)S(1)}, f32[640]{0:T(1024)}, u32[]{:S(2)}) copy-start(f32[640]{0:T(1024)} %shift_ref.1) | copy-start | bytes 7684
  89.6 21.9 %collective-permute-start.13 = (f32[64,1280]{1,0:T(8,128)S(1)}, f32[64,1280]{1,0:T(8,128)S(1)}, u32[]{:S(2)}, u32[]{:S(2)}) collective-permute-start(f32[64,1280]{1,0:T(8,128)S(1)} %get-tuple-element.54), channel_id=1, source_target_pairs={{0,1},{1,2},{2,3},{3,4},{4,5},{5,6},{6,7},{7,8},{8,9},{9,10},{10,1... | collective-permute-start | bytes 983048 | tf_op jit(solution)/shard_map/ppermute | solution.py:466
  93.9 17.6 %collective-permute-start.14 = (f32[64,1280]{1,0:T(8,128)S(1)}, f32[64,1280]{1,0:T(8,128)S(1)}, u32[]{:S(2)}, u32[]{:S(2)}) collective-permute-start(f32[64,1280]{1,0:T(8,128)S(1)} %get-tuple-element.53), channel_id=1, source_target_pairs={{1,0},{2,1},{3,2},{4,3},{5,4},{6,5},{7,6},{8,7},{9,8},{10,9},{11,1... | collective-permute-start | bytes 983048 | tf_op jit(solution)/shard_map/ppermute | solution.py:467
